TPU v7x, 32 devices: a whole 2x2x4 slice. The times are simulated.
32 devices in a mesh: dp: 32 (over z, y, x, core).
Axes of the slice: x: 2, y: 2, z: 4, core: 2. Of those that a mesh axis runs over, the one named last changes fastest.
Arguments:
- tokens: bfloat16 [65536, 768], P('dp'), may hold values from -6 to 6
- eigvecs: float32 [512, 128, 16], P('dp'), may hold values from -6 to 6
- counts: int32 [512, 2], P('dp'), may hold values from 16 to 84, as said below
- endpoints: int32 [512, 128, 2], P('dp'), may hold values from 0 to 41, as said below
- cotangent: bfloat16 [65536, 768], P('dp'), may hold values from -80 to 80
- attend_in: float32 [768, 2304], P('dp'), may hold values from -0.21875 to 0.21875
- attend_in_first: float32 [768, 2304], P('dp'), may hold values from -0.00036621094 to 0.00036621094
- attend_in_second: float32 [768, 2304], P('dp'), may hold values from 2.7995772e-10 to 1.1198309e-09
- attend_out: float32 [768, 768], P(None, 'dp'), may hold values from -1.75 to 1.75
- attend_out_first: float32 [768, 768], P(None, 'dp'), may hold values from -0.00036621094 to 0.00036621094
- attend_out_second: float32 [768, 768], P(None, 'dp'), may hold values from 2.7995772e-10 to 1.1198309e-09
- feed_up: float32 [768, 768], P('dp'), may hold values from -0.21875 to 0.21875
- feed_up_first: float32 [768, 768], P('dp'), may hold values from -0.00036621094 to 0.00036621094
- feed_up_second: float32 [768, 768], P('dp'), may hold values from 2.7995772e-10 to 1.1198309e-09
- feed_down: float32 [768, 768], P(None, 'dp'), may hold values from -0.21875 to 0.21875
- feed_down_first: float32 [768, 768], P(None, 'dp'), may hold values from -0.00036621094 to 0.00036621094
- feed_down_second: float32 [768, 768], P(None, 'dp'), may hold values from 2.7995772e-10 to 1.1198309e-09
- label_in: float32 [32, 768], P(None, 'dp'), may hold values from -1 to 1
- label_in_first: float32 [32, 768], P(None, 'dp'), may hold values from -0.00036621094 to 0.00036621094
- label_in_second: float32 [32, 768], P(None, 'dp'), may hold values from 2.7995772e-10 to 1.1198309e-09
- vectors: float32 [11, 768], P(None, 'dp'), may hold values from -6 to 6, as said below
- vectors_first: float32 [11, 768], P(None, 'dp'), may hold values from -0.00036621094 to 0.00036621094
- vectors_second: float32 [11, 768], P(None, 'dp'), may hold values from 2.7995772e-10 to 1.1198309e-09
- step_count: int32 [], replicated, may hold values from 2 to 21
- learn_rate: float32 [], replicated, may hold values from 0.2 to 0.4
Outputs:
- layer_out: bfloat16 [65536, 768], P('dp')
- tokens_grad: float32 [65536, 768], P('dp')
- grad_norm: float32 [], replicated
- attend_in_grad: float32 [768, 2304], P('dp')
- attend_in_first_new: float32 [768, 2304], P('dp')
- attend_in_second_new: float32 [768, 2304], P('dp')
- attend_in_new: float32 [768, 2304], P('dp')
- attend_out_grad: float32 [768, 768], P(None, 'dp')
- attend_out_first_new: float32 [768, 768], P(None, 'dp')
- attend_out_second_new: float32 [768, 768], P(None, 'dp')
- attend_out_new: float32 [768, 768], P(None, 'dp')
- feed_up_grad: float32 [768, 768], P('dp')
- feed_up_first_new: float32 [768, 768], P('dp')
- feed_up_second_new: float32 [768, 768], P('dp')
- feed_up_new: float32 [768, 768], P('dp')
- feed_down_grad: float32 [768, 768], P(None, 'dp')
- feed_down_first_new: float32 [768, 768], P(None, 'dp')
- feed_down_second_new: float32 [768, 768], P(None, 'dp')
- feed_down_new: float32 [768, 768], P(None, 'dp')
- label_in_grad: float32 [32, 768], P(None, 'dp')
- label_in_first_new: float32 [32, 768], P(None, 'dp')
- label_in_second_new: float32 [32, 768], P(None, 'dp')
- label_in_new: float32 [32, 768], P(None, 'dp')
- vectors_grad: float32 [11, 768], P(None, 'dp')
- vectors_first_new: float32 [11, 768], P(None, 'dp')
- vectors_second_new: float32 [11, 768], P(None, 'dp')
- vectors_new: float32 [11, 768], P(None, 'dp')
Inputs may be any that keep to these rules, and one draw needn't show every extreme that they name: `counts`: row m holds molecule m's node count and then its edge count; the edge count lies between the node count and twice it. `endpoints`: entry j of a molecule holds two different nodes below its node count; entries at or beyond its edge count are not used. `vectors`: rows 0 and 5 are positive.
All inputs are finite; a program needn't handle non-finite values.
Results may differ from a plain program's by a relative error of at most 0.012.
The roundings to bfloat16 on the way count: a program that leaves them out, or rounds other values in their place, can miss the bound.
Values may be sent and summed in bfloat16 or wider, within the bound.
A program may use at most 192 MiB of HBM per device.

v0:
```python
import jax
import jax.numpy as jnp
from jax import lax
from jax.sharding import PartitionSpec as P

HEADS = 32


EPS_NORM = 1e-05
MASK_FILL = -1000000000.0
SQRT_HALF = 0.7071067811865476
INV_SQRT_TWO_PI = 0.3989422804014327
BETA_ONE = 0.9
BETA_TWO = 0.999
ADAM_EPS = 1e-08
DECAY_RATE = 0.01
CLIP_LIMIT = 1.0
NORM_EPS = 1e-06


def contract_rows(left_side, right_side):
    return lax.dot_general(
        left_side, right_side, (((0,), (0,)), ((), ())), preferred_element_type=jnp.float32
    )


def times_transposed(left_side, right_side):
    return lax.dot_general(
        left_side, right_side, (((1,), (1,)), ((), ())), preferred_element_type=jnp.float32
    )


def gelu_exact(values):
    return values * 0.5 * (1.0 + lax.erf(values * SQRT_HALF))


def gelu_slope(values):
    return (
        0.5 * (1.0 + lax.erf(values * SQRT_HALF))
        + values * jnp.exp(-0.5 * values * values) * INV_SQRT_TWO_PI
    )


def layer_stats(values):
    centred = values - jnp.mean(values, -1, keepdims=True)
    recip_std = lax.rsqrt(jnp.mean(centred * centred, -1, keepdims=True) + EPS_NORM)
    return (centred * recip_std, recip_std)


def norm_back(grad_out, normed, recip_std, gain_row):
    scaled = grad_out * gain_row
    return recip_std * (
        scaled
        - jnp.mean(scaled, -1, keepdims=True)
        - normed * jnp.mean(scaled * normed, -1, keepdims=True)
    )


def identifiers(eigvecs, counts, endpoints):
    mol_count, seq_len = (endpoints.shape[0], endpoints.shape[1])
    places = jnp.arange(seq_len, dtype=jnp.int32)[None, :]
    node_count = counts[:, 0:1]
    edge_count = counts[:, 1:2]
    is_node = places < node_count
    is_edge = jnp.logical_and(places >= node_count, places < node_count + edge_count)
    edge_slot = jnp.clip(places - node_count, 0, seq_len - 1)
    first_end = jnp.take_along_axis(endpoints[:, :, 0], edge_slot, 1)
    second_end = jnp.take_along_axis(endpoints[:, :, 1], edge_slot, 1)
    source = jnp.where(is_node, places, first_end)
    target = jnp.where(is_node, places, second_end)
    left_half = jnp.take_along_axis(eigvecs, source[:, :, None], 1)
    right_half = jnp.take_along_axis(eigvecs, target[:, :, None], 1)
    is_live = jnp.logical_or(is_node, is_edge)
    labels = jnp.concatenate([left_half, right_half], -1) * is_live[:, :, None].astype(jnp.float32)
    return (
        labels.reshape(mol_count * seq_len, -1),
        is_node.reshape(-1).astype(jnp.float32),
        is_edge.reshape(-1).astype(jnp.float32),
        is_live,
    )


def masked_scores(queries, key_heads, is_live):
    score_scale = queries.shape[-1] ** (-0.5)
    scores = (
        jnp.einsum("mqhd,mkhd->mhqk", queries, key_heads, preferred_element_type=jnp.float32)
        * score_scale
    )
    return jnp.where(is_live[:, None, None, :], scores, MASK_FILL)


def attend_block(pieces):
    queries, key_heads, value_heads, is_live = pieces
    scores = masked_scores(queries, key_heads, is_live)
    maxima = jnp.max(scores, -1, keepdims=True)
    exponent = jnp.exp(scores - maxima)
    totals = jnp.sum(exponent, -1, keepdims=True)
    shares = (exponent / totals).astype(jnp.bfloat16)
    attended = jnp.einsum(
        "mhqk,mkhd->mqhd", shares, value_heads, preferred_element_type=jnp.float32
    )
    return (attended.astype(jnp.bfloat16), maxima + jnp.log(totals))


def attend_back(pieces):
    queries, key_heads, value_heads, is_live, log_total, grad_heads = pieces
    score_scale = queries.shape[-1] ** (-0.5)
    shares = jnp.exp(masked_scores(queries, key_heads, is_live) - log_total)
    grad_shares = jnp.einsum(
        "mqhd,mkhd->mhqk", grad_heads, value_heads, preferred_element_type=jnp.float32
    )
    inner_sum = jnp.sum(shares * grad_shares, -1, keepdims=True)
    grad_scores = (shares * (grad_shares - inner_sum)).astype(jnp.bfloat16)
    grad_value = jnp.einsum(
        "mhqk,mqhd->mkhd",
        shares.astype(jnp.bfloat16),
        grad_heads,
        preferred_element_type=jnp.float32,
    )
    grad_query = (
        jnp.einsum("mhqk,mkhd->mqhd", grad_scores, key_heads, preferred_element_type=jnp.float32)
        * score_scale
    )
    grad_key = (
        jnp.einsum("mhqk,mqhd->mkhd", grad_scores, queries, preferred_element_type=jnp.float32)
        * score_scale
    )
    return (grad_query, grad_key, grad_value)


def adam_update(master, first_old, second_old, gradient, step_f, learn_rate, decay_flag):
    first_new = BETA_ONE * first_old + (1.0 - BETA_ONE) * gradient
    second_new = BETA_TWO * second_old + (1.0 - BETA_TWO) * gradient * gradient
    moment_hat = first_new / (1.0 - BETA_ONE**step_f)
    second_hat = second_new / (1.0 - BETA_TWO**step_f)
    change = moment_hat / (jnp.sqrt(second_hat) + ADAM_EPS)
    if decay_flag:
        change = change + DECAY_RATE * master
    return (first_new, second_new, master - learn_rate * change)


def body(
    tokens,
    eigvecs,
    counts,
    endpoints,
    cotangent,
    attend_in,
    attend_in_first,
    attend_in_second,
    attend_out,
    attend_out_first,
    attend_out_second,
    feed_up,
    feed_up_first,
    feed_up_second,
    feed_down,
    feed_down_first,
    feed_down_second,
    label_in,
    label_in_first,
    label_in_second,
    vectors,
    vectors_first,
    vectors_second,
    step_count,
    learn_rate,
):
    copy_in = attend_in.astype(jnp.bfloat16)
    copy_out = attend_out.astype(jnp.bfloat16)
    copy_up = feed_up.astype(jnp.bfloat16)
    copy_down = feed_down.astype(jnp.bfloat16)
    copy_label = label_in.astype(jnp.bfloat16)
    copy_vectors = vectors.astype(jnp.bfloat16)
    gathered = (
        lax.all_gather(copy_in, "dp", axis=0, tiled=True),
        lax.all_gather(copy_out, "dp", axis=1, tiled=True),
        lax.all_gather(copy_up, "dp", axis=0, tiled=True),
        lax.all_gather(copy_down, "dp", axis=1, tiled=True),
        lax.all_gather(copy_label, "dp", axis=1, tiled=True),
        lax.all_gather(copy_vectors, "dp", axis=1, tiled=True),
    )
    weight_in, weight_out, weight_up, weight_down, weight_label, vector_low = gathered
    vector_rows = vector_low.astype(jnp.float32)
    model_width = weight_out.shape[0]
    mol_count, seq_len = (endpoints.shape[0], endpoints.shape[1])
    block_mols = min(mol_count, max(1, 512 // seq_len))
    blocks = mol_count // block_mols
    labels, is_node, is_edge, is_live = identifiers(eigvecs, counts, endpoints)
    label_low = labels.astype(jnp.bfloat16)
    tokens_f = tokens.astype(jnp.float32)
    embedded = (
        tokens_f
        + jnp.dot(label_low, weight_label, preferred_element_type=jnp.float32)
        + is_node[:, None] * vector_rows[9]
        + is_edge[:, None] * vector_rows[10]
    )
    normed_one, recip_one = layer_stats(embedded)
    input_one = (normed_one * vector_rows[0] + vector_rows[1]).astype(jnp.bfloat16)
    bias_row = jnp.concatenate([vector_rows[2], jnp.zeros_like(vector_rows[2]), vector_rows[3]])
    projected = (
        jnp.dot(input_one, weight_in, preferred_element_type=jnp.float32) + bias_row
    ).astype(jnp.bfloat16)

    def to_heads(columns):
        return columns.reshape(blocks, block_mols, seq_len, HEADS, -1)

    queries = to_heads(projected[:, :model_width])
    key_heads = to_heads(projected[:, model_width : 2 * model_width])
    value_heads = to_heads(projected[:, 2 * model_width :])
    live_blocks = is_live.reshape(blocks, block_mols, seq_len)
    attended_blocks, log_totals = lax.map(
        attend_block, (queries, key_heads, value_heads, live_blocks)
    )
    attended = attended_blocks.reshape(-1, model_width)
    middle = embedded + (
        jnp.dot(attended, weight_out, preferred_element_type=jnp.float32) + vector_rows[4]
    )
    normed_two, recip_two = layer_stats(middle)
    input_two = (normed_two * vector_rows[5] + vector_rows[6]).astype(jnp.bfloat16)
    pre_act = jnp.dot(input_two, weight_up, preferred_element_type=jnp.float32) + vector_rows[7]
    activated = gelu_exact(pre_act).astype(jnp.bfloat16)
    layer_out = (
        middle
        + (jnp.dot(activated, weight_down, preferred_element_type=jnp.float32) + vector_rows[8])
    ).astype(jnp.bfloat16)
    regathered = (
        lax.all_gather(copy_in, "dp", axis=0, tiled=True),
        lax.all_gather(copy_out, "dp", axis=1, tiled=True),
        lax.all_gather(copy_up, "dp", axis=0, tiled=True),
        lax.all_gather(copy_down, "dp", axis=1, tiled=True),
        lax.all_gather(copy_label, "dp", axis=1, tiled=True),
        lax.all_gather(copy_vectors, "dp", axis=1, tiled=True),
    )
    weight_in, weight_out, weight_up, weight_down, weight_label, vector_low = regathered
    vector_rows = vector_low.astype(jnp.float32)
    back_f = cotangent.astype(jnp.float32)
    grad_down = contract_rows(activated, cotangent)
    grad_down_bias = jnp.sum(back_f, 0)
    grad_act = times_transposed(cotangent, weight_down)
    grad_pre = (grad_act * gelu_slope(pre_act)).astype(jnp.bfloat16)
    grad_up = contract_rows(input_two, grad_pre)
    grad_up_bias = jnp.sum(grad_pre, 0, dtype=jnp.float32)
    grad_in_two = times_transposed(grad_pre, weight_up)
    grad_gain_two = jnp.sum(grad_in_two * normed_two, 0)
    grad_shift_two = jnp.sum(grad_in_two, 0)
    grad_middle = back_f + norm_back(grad_in_two, normed_two, recip_two, vector_rows[5])
    branch_low = grad_middle.astype(jnp.bfloat16)
    grad_out = contract_rows(attended, branch_low)
    grad_out_bias = jnp.sum(branch_low, 0, dtype=jnp.float32)
    grad_attended = times_transposed(branch_low, weight_out).astype(jnp.bfloat16)
    grad_query, grad_key, grad_value = lax.map(
        attend_back,
        (queries, key_heads, value_heads, live_blocks, log_totals, to_heads(grad_attended)),
    )
    grad_proj = jnp.concatenate(
        [
            grad_query.reshape(-1, model_width),
            grad_key.reshape(-1, model_width),
            grad_value.reshape(-1, model_width),
        ],
        1,
    ).astype(jnp.bfloat16)
    grad_in = contract_rows(input_one, grad_proj)
    grad_query_bias = jnp.sum(grad_proj[:, :model_width], 0, dtype=jnp.float32)
    grad_value_bias = jnp.sum(grad_proj[:, 2 * model_width :], 0, dtype=jnp.float32)
    grad_in_one = times_transposed(grad_proj, weight_in)
    grad_gain_one = jnp.sum(grad_in_one * normed_one, 0)
    grad_shift_one = jnp.sum(grad_in_one, 0)
    tokens_grad = grad_middle + norm_back(grad_in_one, normed_one, recip_one, vector_rows[0])
    grad_label = contract_rows(label_low, tokens_grad.astype(jnp.bfloat16))
    grad_node = jnp.sum(tokens_grad * is_node[:, None], 0)
    grad_edge = jnp.sum(tokens_grad * is_edge[:, None], 0)
    grad_vectors = jnp.stack(
        [
            grad_gain_one,
            grad_shift_one,
            grad_query_bias,
            grad_value_bias,
            grad_out_bias,
            grad_gain_two,
            grad_shift_two,
            grad_up_bias,
            grad_down_bias,
            grad_node,
            grad_edge,
        ]
    )
    summed_in, summed_out, summed_up, summed_down, summed_label, summed_vectors = (
        lax.psum_scatter(grad_in, "dp", scatter_dimension=0, tiled=True),
        lax.psum_scatter(grad_out, "dp", scatter_dimension=1, tiled=True),
        lax.psum_scatter(grad_up, "dp", scatter_dimension=0, tiled=True),
        lax.psum_scatter(grad_down, "dp", scatter_dimension=1, tiled=True),
        lax.psum_scatter(grad_label, "dp", scatter_dimension=1, tiled=True),
        lax.psum_scatter(grad_vectors, "dp", scatter_dimension=1, tiled=True),
    )
    summed = (summed_in, summed_out, summed_up, summed_down, summed_label, summed_vectors)
    local_squares = sum((jnp.sum(summed_part * summed_part) for summed_part in summed))
    grad_norm = jnp.sqrt(lax.psum(local_squares, "dp"))
    factor = jnp.minimum(1.0, CLIP_LIMIT / (grad_norm + NORM_EPS))
    step_f = step_count.astype(jnp.float32)
    masters = (attend_in, attend_out, feed_up, feed_down, label_in, vectors)
    firsts = (
        attend_in_first,
        attend_out_first,
        feed_up_first,
        feed_down_first,
        label_in_first,
        vectors_first,
    )
    seconds = (
        attend_in_second,
        attend_out_second,
        feed_up_second,
        feed_down_second,
        label_in_second,
        vectors_second,
    )
    results = []
    for position in range(6):
        clipped = summed[position] * factor
        first_new, second_new, master_new = adam_update(
            masters[position],
            firsts[position],
            seconds[position],
            clipped,
            step_f,
            learn_rate,
            position < 5,
        )
        results.append((clipped, first_new, second_new, master_new))
    return (
        layer_out,
        tokens_grad,
        grad_norm,
        results[0][0],
        results[0][1],
        results[0][2],
        results[0][3],
        results[1][0],
        results[1][1],
        results[1][2],
        results[1][3],
        results[2][0],
        results[2][1],
        results[2][2],
        results[2][3],
        results[3][0],
        results[3][1],
        results[3][2],
        results[3][3],
        results[4][0],
        results[4][1],
        results[4][2],
        results[4][3],
        results[5][0],
        results[5][1],
        results[5][2],
        results[5][3],
    )


def solution(mesh):
    placed = (
        P("dp", None),
        P("dp", None, None),
        P("dp", None),
        P("dp", None, None),
        P("dp", None),
        P("dp", None),
        P("dp", None),
        P("dp", None),
        P(None, "dp"),
        P(None, "dp"),
        P(None, "dp"),
        P("dp", None),
        P("dp", None),
        P("dp", None),
        P(None, "dp"),
        P(None, "dp"),
        P(None, "dp"),
        P(None, "dp"),
        P(None, "dp"),
        P(None, "dp"),
        P(None, "dp"),
        P(None, "dp"),
        P(None, "dp"),
        P(),
        P(),
    )
    return jax.shard_map(
        body,
        mesh=mesh,
        in_specs=placed,
        out_specs=(
            P("dp", None),
            P("dp", None),
            P(),
            P("dp", None),
            P("dp", None),
            P("dp", None),
            P("dp", None),
            P(None, "dp"),
            P(None, "dp"),
            P(None, "dp"),
            P(None, "dp"),
            P("dp", None),
            P("dp", None),
            P("dp", None),
            P("dp", None),
            P(None, "dp"),
            P(None, "dp"),
            P(None, "dp"),
            P(None, "dp"),
            P(None, "dp"),
            P(None, "dp"),
            P(None, "dp"),
            P(None, "dp"),
            P(None, "dp"),
            P(None, "dp"),
            P(None, "dp"),
            P(None, "dp"),
        ),
        check_vma=False,
    )
```

profile of v0, /device:TPU:0, one launch (start us, length us, event | category | flops | bytes accessed | tf_op | source)
XLA Modules:
  0.0 1106.0 jit_solution(928500774559968737)
XLA Ops:
  15.3 13.1 %gather_fusion = s32[2048]{0:T(1024)S(1)} fusion(s32[16,128]{1,0:T(8,128)S(1)} %bitcast.215, s32[2048]{0:T(1024)S(1)} %fusion.58), kind=kCustom, calls=%fused_computation.clone | custom fusion | bytes 32768 | tf_op jit(solution)/shard_map/jit(take_along_axis)/gather | solution.py:67
  28.4 13.1 %gather_fusion.2 = s32[2048]{0:T(1024)S(1)} fusion(s32[16,128]{1,0:T(8,128)S(1)} %bitcast.214, s32[2048]{0:T(1024)S(1)} %fusion.58), kind=kCustom, calls=%fused_computation.2.clone | custom fusion | bytes 32768 | tf_op jit(solution)/shard_map/jit(take_along_axis)/gather | solution.py:68
  42.0 43.7 %all-gather = bf16[32,24,11]{1,2,0:T(8,128)(2,1)S(1)} all-gather(bf16[1,24,11]{1,2,0:T(8,128)(2,1)S(1)} %convert_bitcast_fusion.3), channel_id=1, replica_groups=mesh['dp'=32] {'dp'}, dimensions={0}, use_global_device_ids=true | all-gather | bytes 17424 | tf_op jit(solution)/shard_map/all_gather | solution.py:181
  86.8 39.8 %all_gather.23 = bf16[32,768]{0,1:T(8,128)(2,1)} all-gather(bf16[32,24]{0,1:T(8,128)(2,1)S(1)} %convert_element_type.124), channel_id=1, replica_groups=mesh['dp'=32] {'dp'}, dimensions={1}, use_global_device_ids=true | all-gather | bytes 50688 | tf_op jit(solution)/shard_map/all_gather | solution.py:180
  126.9 13.3 %gather_fusion.3 = f32[2048,16]{1,0:T(8,128)S(1)} fusion(f32[16,128,16]{2,1,0:T(8,128)S(1)} %copy.151, s32[2048]{0:T(1024)S(1)} %get-tuple-element.402), kind=kCustom, calls=%fused_computation.3.clone | custom fusion | bytes 278528 | tf_op jit(solution)/shard_map/jit(take_along_axis)/gather | solution.py:72
  140.2 13.0 %gather_fusion.1 = f32[2048,16]{1,0:T(8,128)S(1)} fusion(f32[16,128,16]{2,1,0:T(8,128)S(1)} %copy.151, s32[2048]{0:T(1024)S(1)} %get-tuple-element.401), kind=kCustom, calls=%fused_computation.1.clone | custom fusion | bytes 278528 | tf_op jit(solution)/shard_map/jit(take_along_axis)/gather | solution.py:71
  156.6 4.7 copy.149
  161.3 3.8 fusion.82
  171.7 11.4 %add_convert_fusion = bf16[2048,2304]{1,0:T(8,128)(2,1)S(1)} fusion(bf16[768,2304]{1,0:T(8,128)(2,1)} %all-gather.6.cloned.1.call-done, f32[2304]{0:T(1024)S(1)} %pad_maximum_fusion, f32[2048,768]{0,1:T(8,128)} %copy-done.3, f32[768]{0:T(1024)S(1)} %get-tuple-element.317, f32[768]{0:T(1024)S(1)} %get-tuple-element.318, f32[2048]{0:T(1024)S(1)} %add_rsqrt_fusion.1, ...), kind=kOutput, calls=%fused_computation.58 | convolution fusion | flops 7265058816 | bytes 19299328 | tf_op jit(solution)/shard_map/dot_general | solution.py:202
  189.2 6.1 reshape.298
  198.0 4.7 copy.159
  202.7 6.3 reshape.297
  209.0 4.4 copy.162
  213.3 4.6 copy.158
  217.9 6.1 reshape.296
  224.1 4.4 copy.161
  228.4 43.2 %while.26 = (s32[]{:T(128)}, bf16[4,4,128,32,24]{2,1,0,4,3:T(4,128)(2,1)}, f32[4,4,32,128,1]{3,2,1,4,0:T(8,128)S(1)}, bf16[4,4,128,32,24]{2,4,3,1,0:T(8,128)(2,1...) while((s32[]{:T(128)}, ...), condition=%wide.region_5.8_spmd, body=%wide.region_2.0_spmd.sunk | while | flops 226869248 | bytes 30412396 | solution.py:212
  228.4 3.5 fusion.125
  234.4 3.2 fusion.127
  239.2 3.5 fusion.125
  250.1 3.5 fusion.125
  260.9 3.5 fusion.125
  271.6 7.0 reshape.299
  278.7 6.7 fusion.83
  290.7 7.6 multiply_convert_fusion.1
  298.3 7.3 convert_reduce_fusion.1
  305.6 5.1 fusion.85
  310.8 6.7 copy.168
  317.5 7.2 multiply_reduce_fusion.3
  325.2 5.8 convert_reduce_fusion.2
  333.7 4.2 convolution_convert_fusion
  337.9 4.9 copy.169
  342.8 6.1 reshape.300
  348.9 86.2 %while.27 = (s32[]{:T(128)}, bf16[4,4,128,32,24]{2,4,3,1,0:T(8,128)(2,1)}, bf16[4,4,128,32,24]{2,4,3,1,0:T(8,128)(2,1)}, bf16[4,4,128,32,24]{2,4,3,1,0:T(8,128)(...) while((s32[]{:T(128)}, ...), condition=%wide.region_12.15_spmd, body=%wide.region_10.14_spmd.sunk | while | flops 535543808 | bytes 150673232 | solution.py:252
  355.6 4.5 multiply_reduce_fusion.18
  363.3 3.8 bitcast_dynamic-update-slice_fusion.10
  377.1 4.5 multiply_reduce_fusion.18
  384.8 3.8 bitcast_dynamic-update-slice_fusion.10
  398.5 4.5 multiply_reduce_fusion.18
  406.2 3.8 bitcast_dynamic-update-slice_fusion.10
  420.0 4.5 multiply_reduce_fusion.18
  427.7 3.8 bitcast_dynamic-update-slice_fusion.10
  435.0 6.0 copy.176
  441.0 4.8 reshape.303
  445.8 7.1 copy.174
  452.9 6.2 reshape.301
  459.1 6.0 copy.175
  465.1 6.1 reshape.302
  476.0 9.8 fusion.84
  485.9 6.7 copy.177
  492.6 6.6 multiply_reduce_fusion.4
  500.3 5.5 multiply_reduce_fusion.1
  510.3 7.0 fusion.86
  517.6 6.0 fusion.87
  523.7 7.9 fusion.66
  531.6 14.5 %fusion.73 = f32[768,2304]{1,0:T(8,128)} fusion(bf16[2048,2304]{0,1:T(8,128)(2,1)} %copy-done.20, f32[2048,768]{0,1:T(8,128)} %copy-done.3, f32[768]{0:T(1024)S(1)} %copy-done.56, f32[768]{0:T(1024)S(1)} %copy-done.40, f32[2048]{0:T(1024)S(1)} %copy-done.34, f32[2048]{0:T(1024)S(1)} %copy-done.31), kind=kOutput, calls=%fused_computation.197 | convolution fusion | flops 7255621632 | bytes 22829056 | tf_op jit(solution)/shard_map/dot_general | solution.py:22
  547.6 6.7 copy.181
  557.5 37.7 %all-reduce.1 = f32[11,768]{1,0:T(8,128)S(1)} all-reduce(f32[11,768]{1,0:T(8,128)S(1)} %stack.47), channel_id=7, replica_groups=mesh['dp'=32] {'dp'}, use_global_device_ids=true, to_apply=%region_36.39.clone | all-reduce | flops 8448 | bytes 67584
  595.9 6.8 add_convert_fusion.1
  604.2 102.7 %reduce-scatter.13.cloned.1.call-done = f32[24,768]{1,0:T(8,128)} async-done(((f32[768,768]{1,0:T(8,128)}), f32[24,768]{1,0:T(8,128)}) %reduce-scatter.13.cloned.1.call-update) | async-done | bytes 73744 | tf_op jit(solution)/shard_map/reduce_scatter | solution.py:292
  708.4 101.9 %reduce-scatter.15.cloned.1.call-done = f32[768,24]{0,1:T(8,128)} async-done(((f32[768,768]{0,1:T(8,128)}), f32[768,24]{0,1:T(8,128)}) %reduce-scatter.15.cloned.1.call-update) | async-done | bytes 73744 | tf_op jit(solution)/shard_map/reduce_scatter | solution.py:293
  811.8 103.3 %reduce-scatter.11.cloned.1.call-done = f32[768,24]{0,1:T(8,128)} async-done(((f32[768,768]{0,1:T(8,128)}), f32[768,24]{0,1:T(8,128)}) %reduce-scatter.11.cloned.1.call-update) | async-done | bytes 73744 | tf_op jit(solution)/shard_map/reduce_scatter | solution.py:291
  916.6 122.4 %reduce-scatter.9.cloned.1.call-done = f32[24,2304]{1,0:T(8,128)} async-done(((f32[768,2304]{1,0:T(8,128)}), f32[24,2304]{1,0:T(8,128)}) %reduce-scatter.9.cloned.1.call-update) | async-done | bytes 221200 | tf_op jit(solution)/shard_map/reduce_scatter | solution.py:290
  1047.4 40.0 %psum.7 = f32[]{:T(128)} all-reduce(f32[]{:T(128)S(6)} %add.284), channel_id=1, replica_groups=mesh['dp'=32] {'dp'}, use_global_device_ids=true, to_apply=%region_38.41 | all-reduce | flops 1 | bytes 8 | tf_op jit(solution)/shard_map/psum | solution.py:299
  (320 shorter events, 150.0 us)
Async XLA Ops:
  7.2 164.5 %all-gather.6.cloned.1.call-start = ((), (), s32[]{:S(2)}) async-start(), calls=%async_computation.5 | async-start | bytes 3649536 | tf_op jit(solution)/shard_map/all_gather | solution.py:176
  8.9 269.8 %all-gather.8.cloned.1.call-start = ((), (), s32[]{:S(2)}) async-start(), calls=%async_computation.6 | async-start | bytes 1216512 | tf_op jit(solution)/shard_map/all_gather | solution.py:177
  10.4 280.3 %all-gather.10.cloned.1.call-start = ((), (), s32[]{:S(2)}) async-start(), calls=%async_computation.7 | async-start | bytes 1216512 | tf_op jit(solution)/shard_map/all_gather | solution.py:178
  12.0 286.3 %all-gather.12.cloned.1.call-start = ((), (), s32[]{:S(2)}) async-start(), calls=%async_computation.8 | async-start | bytes 1216512 | tf_op jit(solution)/shard_map/all_gather | solution.py:179
  13.6 589.2 %reduce-scatter.17.cloned.1.call-start = ((), (), s32[]{:S(2)}) async-start(), calls=%async_computation.13 | async-start | bytes 405504
  28.4 13.5 %copy-start.47 = (f32[11,24]{1,0:T(8,128)S(1)}, f32[11,24]{1,0:T(8,128)}, u32[]{:S(2)}) copy-start(f32[11,24]{1,0:T(8,128)} %param.53) | copy-start | bytes 3172
  28.4 13.5 %copy-start.36 = (f32[32,24]{0,1:T(8,128)S(1)}, f32[32,24]{0,1:T(8,128)}, u32[]{:S(2)}) copy-start(f32[32,24]{0,1:T(8,128)} %param.50) | copy-start | bytes 9220
  28.4 98.2 %copy-start.29 = (f32[16,128,16]{1,2,0:T(8,128)S(1)}, f32[16,128,16]{1,2,0:T(8,128)}, u32[]{:S(2)}) copy-start(f32[16,128,16]{1,2,0:T(8,128)} %param.34) | copy-start | bytes 393220
  42.0 119.2 %copy-start.41 = (f32[2048]{0:T(1024)}, f32[2048]{0:T(1024)S(1)}, u32[]{:S(2)}) copy-start(f32[2048]{0:T(1024)S(1)} %get-tuple-element.396) | copy-start | bytes 24580
  42.0 119.2 %copy-start.43 = (f32[2048]{0:T(1024)}, f32[2048]{0:T(1024)S(1)}, u32[]{:S(2)}) copy-start(f32[2048]{0:T(1024)S(1)} %get-tuple-element.397) | copy-start | bytes 24580
  42.0 119.2 %copy-start.45 = (f32[2048]{0:T(1024)}, f32[2048]{0:T(1024)S(1)}, u32[]{:S(2)}) copy-start(f32[2048]{0:T(1024)S(1)} %get-tuple-element.398) | copy-start | bytes 24580
  86.8 84.9 %copy-start.39 = (f32[768]{0:T(1024)}, f32[768]{0:T(1024)S(1)}, u32[]{:S(2)}) copy-start(f32[768]{0:T(1024)S(1)} %get-tuple-element.318) | copy-start | bytes 9220
  86.8 84.9 %copy-start.55 = (f32[768]{0:T(1024)}, f32[768]{0:T(1024)S(1)}, u32[]{:S(2)}) copy-start(f32[768]{0:T(1024)S(1)} %get-tuple-element.317) | copy-start | bytes 9220
  156.3 8.9 copy-start.22
  156.6 8.6 copy-start.24
  161.3 7.3 copy-start.11
  165.2 6.5 copy-start.30
  168.6 14.6 %copy-start.33 = (f32[2048]{0:T(1024)}, f32[2048]{0:T(1024)S(1)}, u32[]{:S(2)}) copy-start(f32[2048]{0:T(1024)S(1)} %add_rsqrt_fusion.1) | copy-start | bytes 24580
  217.9 10.5 copy-start.26
  271.6 13.8 %copy-start.1 = (bf16[4,4,128,32,24]{2,4,3,1,0:T(8,128)(2,1)}, bf16[4,4,128,32,24]{2,4,3,1,0:T(8,128)(2,1)S(1)}, u32[]{:S(2)}) copy-start(bf16[4,4,128,32,24]{2,4,3,1,0:T(8,128)(2,1)S(1)} %get-tuple-element.595) | copy-start | bytes 9437188
  286.1 4.6 copy-start.57
  290.7 7.6 copy-start.12
  298.3 7.3 copy-start.62
  305.6 5.2 copy-start.63
  310.8 14.0 %slice-start = ((s8[6291456]{0:T(1024)(128)(4,1)}), s8[2097152]{0:T(1024)(128)(4,1)S(1)}, s32[]{:S(2)}) async-start(s8[6291456]{0:T(1024)(128)(4,1)} %bitcast.216), calls=%async_computation.14 | async-start | bytes 4194304
  317.5 7.2 slice-start.1
  317.5 7.7 copy-start.5
  325.2 8.5 copy-start.61
  337.9 10.9 copy-start.2
  398.5 4.6 copy-start.15
  420.0 4.6 copy-start.15
  445.8 28.5 %copy-start.7 = (bf16[2048,768]{0,1:T(8,128)(2,1)}, bf16[2048,768]{0,1:T(8,128)(2,1)S(1)}, u32[]{:S(2)}) copy-start(bf16[2048,768]{0,1:T(8,128)(2,1)S(1)} %reshape.303) | copy-start | bytes 9437188
  476.0 9.8 copy-start.20
  485.9 6.7 copy-start.31
  485.9 6.7 copy-start.34
  485.9 6.7 copy-start.40
  485.9 13.4 %slice-start.2 = ((s8[6291456]{0:T(1024)(128)(4,1)}), s8[2097152]{0:T(1024)(128)(4,1)S(1)}, s32[]{:S(2)}) async-start(s8[6291456]{0:T(1024)(128)(4,1)} %bitcast.218), calls=%async_computation.16 | async-start | bytes 4194304
  492.6 6.7 slice-start.3
  492.6 7.7 copy-start.6
  492.6 7.7 copy-start.44
  492.6 7.7 copy-start.46
  500.3 8.2 copy-start.23
  500.3 8.2 copy-start.25
  500.3 8.2 copy-start.42
  510.3 7.3 copy-start.13
  510.3 196.6 %reduce-scatter.13.cloned.1.call-start = ((), (), s32[]{:S(2)}) async-start(), calls=%async_computation.11 | async-start | bytes 2433024 | tf_op jit(solution)/shard_map/reduce_scatter | solution.py:292
  517.3 293.0 %reduce-scatter.15.cloned.1.call-start = ((), (), s32[]{:S(2)}) async-start(), calls=%async_computation.12 | async-start | bytes 2433024 | tf_op jit(solution)/shard_map/reduce_scatter | solution.py:293
  523.6 8.0 copy-start.56
  523.6 391.5 %reduce-scatter.11.cloned.1.call-start = ((), (), s32[]{:S(2)}) async-start(), calls=%async_computation.10 | async-start | bytes 2433024 | tf_op jit(solution)/shard_map/reduce_scatter | solution.py:291
  531.6 507.4 %reduce-scatter.9.cloned.1.call-start = ((), (), s32[]{:S(2)}) async-start(), calls=%async_computation.9 | async-start | bytes 7299072 | tf_op jit(solution)/shard_map/reduce_scatter | solution.py:290
  547.6 6.8 copy-start.58
  547.6 6.8 copy-start.59
  547.6 6.8 copy-start.50
  547.6 6.8 copy-start.52
  547.6 6.8 copy-start.51
  547.6 6.8 copy-start.8
  554.4 41.5 %copy-start.54 = (f32[768]{0:T(1024)S(1)}, f32[768]{0:T(1024)}, u32[]{:S(2)}) copy-start(f32[768]{0:T(1024)} %get-tuple-element.310) | copy-start | bytes 9220
  602.7 485.5 %copy-start.48 = (f32[11,24]{1,0:T(8,128)S(1)}, f32[11,24]{1,0:T(8,128)}, u32[]{:S(2)}) copy-start(f32[11,24]{1,0:T(8,128)} %param.53) | copy-start | bytes 3172
  602.7 485.5 %copy-start.53 = (f32[11,24]{1,0:T(8,128)S(1)}, f32[11,24]{1,0:T(8,128)}, u32[]{:S(2)}) copy-start(f32[11,24]{1,0:T(8,128)} %param.55) | copy-start | bytes 3172
  602.7 486.9 %copy-start.37 = (f32[32,24]{0,1:T(8,128)S(1)}, f32[32,24]{0,1:T(8,128)}, u32[]{:S(2)}) copy-start(f32[32,24]{0,1:T(8,128)} %param.50) | copy-start | bytes 9220
  602.7 488.3 %copy-start.27 = (f32[768,24]{0,1:T(8,128)S(1)}, f32[768,24]{0,1:T(8,128)}, u32[]{:S(2)}) copy-start(f32[768,24]{0,1:T(8,128)} %param.47) | copy-start | bytes 221188
  602.7 489.9 %copy-start.28 = (f32[24,768]{1,0:T(8,128)S(1)}, f32[24,768]{1,0:T(8,128)}, u32[]{:S(2)}) copy-start(f32[24,768]{1,0:T(8,128)} %param.44) | copy-start | bytes 221188
  602.8 486.8 %copy-start.38 = (f32[32,24]{0,1:T(8,128)S(1)}, f32[32,24]{0,1:T(8,128)}, u32[]{:S(2)}) copy-start(f32[32,24]{0,1:T(8,128)} %reduce-scatter.17.cloned.1.call-done) | copy-start | bytes 9220
  1039.0 57.0 %copy-start.21 = (f32[24,2304]{1,0:T(8,128)S(1)}, f32[24,2304]{1,0:T(8,128)}, u32[]{:S(2)}) copy-start(f32[24,2304]{1,0:T(8,128)} %reduce-scatter.9.cloned.1.call-done) | copy-start | bytes 663556
  (31 other events, 82.0 us)
Sparse Core Ops, SparseCore 0:
  11.5 63.0 all-gather.5
  78.1 53.0 all-gather.7
  134.7 52.9 all-gather.9
  191.0 52.9 all-gather.11
  510.4 92.3 reduce-scatter.16
  608.8 98.0 reduce-scatter.12
  712.2 98.0 reduce-scatter.14
  817.0 98.0 reduce-scatter.10
  920.8 118.1 reduce-scatter.8
where the time goes:
time: 1110 us
  waiting for transfers between devices  431 us (39%)
  local copies, waits for them, and re-layouts  223 us (20%)
  matrix products  187 us (17%)
  blocking collectives  161 us (15%)
  other arithmetic  81.6 us (7%)
  between operations  22.1 us (2%)
    reduce_scatter x1, waiting for transfers between devices, body(): lax.psum_scatter(grad_in, 'dp', scatter_dimension=0, tiled=True)  122 us
    reduce_scatter x1, waiting for transfers between devices, body(): lax.psum_scatter(grad_out, 'dp', scatter_dimension=1, tiled=True)  103 us
    reduce_scatter x1, waiting for transfers between devices, body(): lax.psum_scatter(grad_up, 'dp', scatter_dimension=0, tiled=True)  103 us
    reduce_scatter x1, waiting for transfers between devices, body(): lax.psum_scatter(grad_down, 'dp', scatter_dimension=1, tiled=True)  102 us
    all_gather x1, blocking collectives, body(): lax.all_gather(copy_vectors, 'dp', axis=1, tiled=True)  43.7 us
    psum x1, blocking collectives, body(): grad_norm = jnp.sqrt(lax.psum(local_squares, 'dp'))  40 us
    all_gather x1, blocking collectives, body(): lax.all_gather(copy_label, 'dp', axis=1, tiled=True)  39.8 us
    unnamed x1, blocking collectives  37.7 us
  transfers between devices with their start and end apart: 9, of which 5 were waited for; matrix products, arithmetic and copies ran while one was open for 23% of the time, Pallas kernels for 0%

commit v1 on v0

v1 whole, which is shorter than its diff:
```python
import functools
import math

import jax
import jax.numpy as jnp
from jax import lax
from jax.experimental import pallas as pl
from jax.experimental.pallas import tpu as pltpu
from jax.sharding import PartitionSpec as P

HEADS = 32
EPS_NORM = 1e-05
MASK_FILL = -1e30
SQRT_HALF = 0.7071067811865476
INV_SQRT_TWO_PI = 0.3989422804014327
BETA_ONE = 0.9
BETA_TWO = 0.999
ADAM_EPS = 1e-08
DECAY_RATE = 0.01
CLIP_LIMIT = 1.0
NORM_EPS = 1e-06
LOG2E = 1.4426950408889634

BF = jnp.bfloat16
F32 = jnp.float32
MESH = pl.DeviceIdType.MESH
LANES = 128
VMEM_LIMIT = 60 << 20

SMALL = 128
NODE, EDGE = 32, 33
GAIN1, SHIFT1, QBIAS, VBIAS, OBIAS, GAIN2, SHIFT2, UBIAS, DBIAS = range(34, 43)


def nn(a, b):
    return lax.dot_general(a, b, (((1,), (0,)), ((), ())), preferred_element_type=F32)


def nt(a, b):
    return lax.dot_general(a, b, (((1,), (1,)), ((), ())), preferred_element_type=F32)


def tn(a, b):
    return lax.dot_general(a, b, (((0,), (0,)), ((), ())), preferred_element_type=F32)


def layer_stats(values):
    centred = values - jnp.mean(values, -1, keepdims=True)
    recip_std = lax.rsqrt(jnp.mean(centred * centred, -1, keepdims=True) + EPS_NORM)
    return centred * recip_std, recip_std


def norm_back(grad_out, normed, recip_std, gain_row):
    scaled = grad_out * gain_row
    return recip_std * (
        scaled
        - jnp.mean(scaled, -1, keepdims=True)
        - normed * jnp.mean(scaled * normed, -1, keepdims=True)
    )


class Heads:
    def __init__(self, width):
        self.dim = width // HEADS
        span = 1
        while (span * self.dim) % LANES:
            span *= 2
        self.block = span
        self.tiles = span * self.dim // LANES
        self.blocks = HEADS // span

    def first(self, head):
        return head * self.dim // LANES

    def last(self, head):
        return ((head + 1) * self.dim - 1) // LANES

    def heads_of(self, tile):
        return [h for h in range(self.block) if self.first(h) <= tile <= self.last(h)]

    def mask(self, tile, head):
        lane = lax.broadcasted_iota(jnp.int32, (1, LANES), 1) + tile * LANES
        inside = jnp.logical_and(lane >= head * self.dim, lane < (head + 1) * self.dim)
        return inside.astype(F32).astype(BF)


def only(value, mask):
    return value * mask


def pair_rows(hd, tiles_of, pair):
    h0, h1 = 2 * pair, 2 * pair + 1
    lo, hi = hd.first(h0), hd.last(h1)
    rows = []
    for h in (h0, h1):
        parts = []
        for t in range(lo, hi + 1):
            if hd.first(h) <= t <= hd.last(h):
                parts.append(only(tiles_of[t], hd.mask(t, h)))
            else:
                parts.append(jnp.zeros_like(tiles_of[t]))
        rows.append(parts[0] if len(parts) == 1 else jnp.concatenate(parts, 1))
    return jnp.concatenate(rows, 0)


def pair_full(hd, tiles_of, pair):
    lo, hi = hd.first(2 * pair), hd.last(2 * pair + 1)
    parts = [tiles_of[t] for t in range(lo, hi + 1)]
    return parts[0] if len(parts) == 1 else jnp.concatenate(parts, 1)


def tile_rows(hd, tile_value, tile):
    return jnp.concatenate([only(tile_value, hd.mask(tile, h)) for h in hd.heads_of(tile)], 0)


def front_kernel(
    counts, tokens, eig, ends, cot, w_in, w_out, w_up, w_down, small,
    out_o, proj_o, lse_o, emb_o, dmid_o, dmix_o, labt_o, gout_o, gup_o, gdown_o, gvec_o,
    small_t, mixed_s, p_buf, acc_out, acc_up, acc_down, acc_vec,
    *, hd, mols, seq, steps,
):
    step = pl.program_id(0)
    width = w_in.shape[0]
    score = hd.dim ** -0.5

    @pl.when(step == 0)
    def _():
        small_t[...] = small[...].astype(F32).T
        acc_out[...] = jnp.zeros_like(acc_out)
        acc_up[...] = jnp.zeros_like(acc_up)
        acc_down[...] = jnp.zeros_like(acc_down)
        acc_vec[...] = jnp.zeros_like(acc_vec)

    row = lambda i: small_t[i : i + 1, :]
    iota0 = lax.broadcasted_iota(jnp.int32, (seq, seq), 0)
    iota1 = lax.broadcasted_iota(jnp.int32, (seq, seq), 1)
    token_row = lax.broadcasted_iota(jnp.int32, (1, seq), 1)
    one = lambda c: c.astype(F32).astype(BF)
    label_rows = []
    for m in range(mols):
        nodes = counts[0, step * mols + m]
        live = nodes + counts[1, step * mols + m]
        eig_f = eig[m]
        eig_low = eig_f.astype(BF)
        shift = one(jnp.logical_and(iota1 - iota0 == nodes, iota1 < live))
        halves = []
        for end in range(2):
            pick = one(iota0 == ends[m, end : end + 1, :])
            edge_lab = nn(eig_low, pick).astype(BF)
            moved = nn(edge_lab, shift)
            halves.append(jnp.where(token_row < nodes, eig_f, moved))
        is_node = (token_row < nodes).astype(F32)
        is_edge = jnp.logical_and(token_row >= nodes, token_row < live).astype(F32)
        kind = jnp.where(lax.broadcasted_iota(jnp.int32, (16, seq), 0) == 0, is_node,
                         jnp.where(lax.broadcasted_iota(jnp.int32, (16, seq), 0) == 1, is_edge, 0.0))
        lab = jnp.concatenate(halves + [kind], 0)
        labt_o[m] = lab.astype(BF)
        pad = jnp.zeros((SMALL - lab.shape[0], seq), F32)
        label_rows.append(jnp.concatenate([lab, pad], 0).T.astype(BF))
    labels = jnp.concatenate(label_rows, 0)
    embedded = tokens[...].astype(F32) + nn(labels, small_t[...].astype(BF))
    emb_o[...] = embedded
    normed, recip = layer_stats(embedded)
    input_one = (normed * row(GAIN1) + row(SHIFT1)).astype(BF)
    for part in range(3):
        cols = slice(part * width, (part + 1) * width)
        value = nn(input_one, w_in[:, cols])
        if part == 0:
            value = value + row(QBIAS)
        if part == 2:
            value = value + row(VBIAS)
        proj_o[:, cols] = value.astype(BF)

    for m in range(mols):
        nodes = counts[0, step * mols + m]
        live = nodes + counts[1, step * mols + m]
        key_live = lax.broadcasted_iota(jnp.int32, (seq, 2 * seq), 0) < live
        rows = slice(m * seq, (m + 1) * seq)
        for b in range(hd.blocks):
            base = b * hd.tiles * LANES
            get = lambda part: [
                proj_o[rows, part * width + base + t * LANES : part * width + base + (t + 1) * LANES]
                for t in range(hd.tiles)
            ]
            q, k, v = get(0), get(1), get(2)
            for pair in range(hd.block // 2):
                scores = nt(pair_full(hd, k, pair), pair_rows(hd, q, pair))
                scores = jnp.where(key_live, scores, MASK_FILL)
                top = jnp.max(scores, 0, keepdims=True)
                ex = jnp.exp2((scores - top) * (score * LOG2E))
                total = jnp.sum(ex, 0, keepdims=True)
                shares = ex * (1.0 / total)
                lse_o[m, b * (hd.block // 2) + pair : b * (hd.block // 2) + pair + 1, :] = (
                    top + jnp.log2(total) * (1.0 / (score * LOG2E))
                )
                for i in range(2):
                    h = 2 * pair + i
                    p_buf[:, h * seq : (h + 1) * seq] = shares[:, i * seq : (i + 1) * seq].T.astype(BF)
            for t in range(hd.tiles):
                hs = hd.heads_of(t)
                mixed = nn(p_buf[:, hs[0] * seq : (hs[-1] + 1) * seq], tile_rows(hd, v[t], t))
                mixed_s[rows, base + t * LANES : base + (t + 1) * LANES] = mixed.astype(BF)

    mixed = mixed_s[...]
    middle = embedded + (nt(mixed, w_out[...]) + row(OBIAS))
    normed2, recip2 = layer_stats(middle)
    input_two = (normed2 * row(GAIN2) + row(SHIFT2)).astype(BF)
    pre = nn(input_two, w_up[...]) + row(UBIAS)
    half_erf = 0.5 * (1.0 + lax.erf(pre * SQRT_HALF))
    act = (pre * half_erf).astype(BF)
    slope = half_erf + pre * jnp.exp(-0.5 * pre * pre) * INV_SQRT_TWO_PI
    out_o[...] = (middle + (nt(act, w_down[...]) + row(DBIAS))).astype(BF)
    back = cot[...]
    back_f = back.astype(F32)
    d_pre_f = nn(back, w_down[...]) * slope
    d_pre = d_pre_f.astype(BF)
    acc_down[...] += tn(back, act)
    acc_up[...] += tn(input_two, d_pre)
    d_in2 = nt(d_pre, w_up[...])
    d_mid = back_f + norm_back(d_in2, normed2, recip2, row(GAIN2))
    dmid_o[...] = d_mid
    branch = d_mid.astype(BF)
    acc_out[...] += tn(branch, mixed)
    dmix_o[...] = nn(branch, w_out[...]).astype(BF)
    add = lambda v: jnp.sum(v, 0, keepdims=True)
    sums = {
        OBIAS: add(branch.astype(F32)),
        GAIN2: add(d_in2 * normed2),
        SHIFT2: add(d_in2),
        UBIAS: add(d_pre.astype(F32)),
        DBIAS: add(back_f),
    }
    for i, v in sums.items():
        acc_vec[i - 34 : i - 33, :] += v

    @pl.when(step == steps - 1)
    def _():
        gout_o[...] = acc_out[...].astype(BF)
        gup_o[...] = acc_up[...].astype(BF)
        gdown_o[...] = acc_down[...].astype(BF)
        gvec_o[...] = acc_vec[...]


def back_kernel(
    counts, proj, lse, emb, dmid, dmix, labt, w_in, small, gvec,
    tg_o, gin_o, gsmall_o,
    small_t, pt_buf, dst_buf, ds_buf, dproj_s, acc_in, acc_vec, acc_lab,
    *, hd, mols, seq, steps,
):
    step = pl.program_id(0)
    width = w_in.shape[0]
    score = hd.dim ** -0.5

    @pl.when(step == 0)
    def _():
        small_t[...] = small[...].astype(F32).T
        acc_in[...] = jnp.zeros_like(acc_in)
        acc_vec[...] = gvec[...]
        acc_lab[...] = jnp.zeros_like(acc_lab)

    row = lambda i: small_t[i : i + 1, :]
    for m in range(mols):
        nodes = counts[0, step * mols + m]
        live = nodes + counts[1, step * mols + m]
        key_live = lax.broadcasted_iota(jnp.int32, (seq, 2 * seq), 0) < live
        rows = slice(m * seq, (m + 1) * seq)
        for b in range(hd.blocks):
            base = b * hd.tiles * LANES
            get = lambda ref, part: [
                ref[rows, part * width + base + t * LANES : part * width + base + (t + 1) * LANES]
                for t in range(hd.tiles)
            ]
            q, k, v, do = get(proj, 0), get(proj, 1), get(proj, 2), get(dmix, 0)
            for pair in range(hd.block // 2):
                scores = nt(pair_full(hd, k, pair), pair_rows(hd, q, pair))
                scores = jnp.where(key_live, scores, MASK_FILL)
                at = b * (hd.block // 2) + pair
                p = jnp.exp2((scores - lse[m, at : at + 1, :]) * (score * LOG2E))
                dp = nt(pair_full(hd, v, pair), pair_rows(hd, do, pair))
                inner = jnp.sum(p * dp, 0, keepdims=True)
                ds = p * (dp - inner)
                cols = slice(2 * pair * seq, (2 * pair + 2) * seq)
                pt_buf[:, cols] = p.astype(BF)
                dst_buf[:, cols] = ds.astype(BF)
                for i in range(2):
                    h = 2 * pair + i
                    ds_buf[:, h * seq : (h + 1) * seq] = ds[:, i * seq : (i + 1) * seq].T.astype(BF)
            for t in range(hd.tiles):
                hs = hd.heads_of(t)
                span = slice(hs[0] * seq, (hs[-1] + 1) * seq)
                at = base + t * LANES
                d_v = nn(pt_buf[:, span], tile_rows(hd, do[t], t))
                d_k = nn(dst_buf[:, span], tile_rows(hd, q[t], t)) * score
                d_q = nn(ds_buf[:, span], tile_rows(hd, k[t], t)) * score
                dproj_s[rows, at : at + LANES] = d_q.astype(BF)
                dproj_s[rows, width + at : width + at + LANES] = d_k.astype(BF)
                dproj_s[rows, 2 * width + at : 2 * width + at + LANES] = d_v.astype(BF)

    normed, recip = layer_stats(emb[...])
    input_one = (normed * row(GAIN1) + row(SHIFT1)).astype(BF)
    d_proj = dproj_s[...]
    acc_in[...] += tn(input_one, d_proj)
    d_in1 = nt(d_proj, w_in[...])
    tg = dmid[...] + norm_back(d_in1, normed, recip, row(GAIN1))
    tg_o[...] = tg
    tg_hi = tg.astype(BF)
    tg_lo = (tg - tg_hi.astype(F32)).astype(BF)
    lab = jnp.concatenate([labt[m] for m in range(mols)], 1)
    acc_lab[...] += nn(lab, tg_hi)
    acc_lab[32:48, :] += nn(lab[32:48, :], tg_lo)
    add = lambda v: jnp.sum(v, 0, keepdims=True)
    sums = {
        GAIN1: add(d_in1 * normed),
        SHIFT1: add(d_in1),
        QBIAS: add(d_proj[:, :width].astype(F32)),
        VBIAS: add(d_proj[:, 2 * width :].astype(F32)),
    }
    for i, v in sums.items():
        acc_vec[i - 34 : i - 33, :] += v

    @pl.when(step == steps - 1)
    def _():
        gin_o[...] = acc_in[...].astype(BF)
        full = jnp.concatenate(
            [acc_lab[0:32, :], acc_lab[32:34, :], acc_vec[0:9, :], jnp.zeros((SMALL - 43, width), F32)], 0
        )
        gsmall_o[...] = full.T.astype(BF)


def whole(shape):
    return pl.BlockSpec(shape, lambda *_: (0,) * len(shape), pipeline_mode=pl.Buffered(1))


def out_whole(shape):
    return pl.BlockSpec(shape, lambda *_: (0,) * len(shape))


def layer(tokens, eig_t, counts_t, ends_t, cot, w_in, w_out, w_up, w_down, small, mols_step):
    count, width = tokens.shape
    mols_all, lap, seq = eig_t.shape
    hd = Heads(width)
    steps = mols_all // mols_step
    rows = mols_step * seq
    tok = lambda w: pl.BlockSpec((rows, w), lambda i, *_: (i, 0))
    mol = lambda a, b: pl.BlockSpec((mols_step, a, b), lambda i, *_: (i, 0, 0))
    params = pltpu.CompilerParams(vmem_limit_bytes=VMEM_LIMIT, dimension_semantics=("arbitrary",))
    sq = (width, width)
    front = pl.pallas_call(
        functools.partial(front_kernel, hd=hd, mols=mols_step, seq=seq, steps=steps),
        grid_spec=pltpu.PrefetchScalarGridSpec(
            num_scalar_prefetch=1,
            grid=(steps,),
            in_specs=[tok(width), mol(lap, seq), mol(2, seq), tok(width), whole((width, 3 * width)),
                      whole(sq), whole(sq), whole(sq), whole((width, SMALL))],
            out_specs=[tok(width), tok(3 * width), mol(HEADS // 2, 2 * seq), tok(width), tok(width), tok(width),
                       mol(48, seq), out_whole(sq), out_whole(sq), out_whole(sq), out_whole((16, width))],
            scratch_shapes=[
                pltpu.VMEM((SMALL, width), F32),
                pltpu.VMEM((rows, width), BF),
                pltpu.VMEM((seq, hd.block * seq), BF),
                pltpu.VMEM(sq, F32), pltpu.VMEM(sq, F32), pltpu.VMEM(sq, F32),
                pltpu.VMEM((16, width), F32),
            ],
        ),
        out_shape=[
            jax.ShapeDtypeStruct((count, width), BF),
            jax.ShapeDtypeStruct((count, 3 * width), BF),
            jax.ShapeDtypeStruct((mols_all, HEADS // 2, 2 * seq), F32),
            jax.ShapeDtypeStruct((count, width), F32),
            jax.ShapeDtypeStruct((count, width), F32),
            jax.ShapeDtypeStruct((count, width), BF),
            jax.ShapeDtypeStruct((mols_all, 48, seq), BF),
            jax.ShapeDtypeStruct(sq, BF),
            jax.ShapeDtypeStruct(sq, BF),
            jax.ShapeDtypeStruct(sq, BF),
            jax.ShapeDtypeStruct((16, width), F32),
        ],
        compiler_params=params,
        name="front",
    )(counts_t, tokens, eig_t, ends_t, cot, w_in, w_out, w_up, w_down, small)
    out, proj, lse, emb, dmid, dmix, labt, g_out, g_up, g_down, g_vec = front
    tg, g_in, g_small = pl.pallas_call(
        functools.partial(back_kernel, hd=hd, mols=mols_step, seq=seq, steps=steps),
        grid_spec=pltpu.PrefetchScalarGridSpec(
            num_scalar_prefetch=1,
            grid=(steps,),
            in_specs=[tok(3 * width), mol(HEADS // 2, 2 * seq), tok(width), tok(width), tok(width), mol(48, seq),
                      whole((width, 3 * width)), whole((width, SMALL)), whole((16, width))],
            out_specs=[tok(width), out_whole((width, 3 * width)), out_whole((width, SMALL))],
            scratch_shapes=[
                pltpu.VMEM((SMALL, width), F32),
                pltpu.VMEM((seq, hd.block * seq), BF),
                pltpu.VMEM((seq, hd.block * seq), BF),
                pltpu.VMEM((seq, hd.block * seq), BF),
                pltpu.VMEM((rows, 3 * width), BF),
                pltpu.VMEM((width, 3 * width), F32),
                pltpu.VMEM((16, width), F32),
                pltpu.VMEM((48, width), F32),
            ],
        ),
        out_shape=[
            jax.ShapeDtypeStruct((count, width), F32),
            jax.ShapeDtypeStruct((width, 3 * width), BF),
            jax.ShapeDtypeStruct((width, SMALL), BF),
        ],
        compiler_params=params,
        name="back",
    )(counts_t, proj, lse, emb, dmid, dmix, labt, w_in, small, g_vec)
    return out, tg, g_in, g_out, g_up, g_down, g_small


class Plan:
    def __init__(self, count):
        self.count = count
        self.bits = count.bit_length() - 1
        self.chip_bits = self.bits - 1
        self.dims = (2,) * self.chip_bits
        near = list(range(1, min(4, self.bits)))
        self.far = list(range(self.bits - 1, near[-1], -1))
        self.turns = [near[i:] + near[:i] for i in range(len(near))]

    def order(self, part):
        return self.far + self.turns[part % len(self.turns)]

    @staticmethod
    def fits(count, rows):
        return count >= 16 and count & (count - 1) == 0 and rows % 8 == 0


def my_place(plan):
    me = lax.axis_index("dp")
    bit = [lax.rem(lax.div(me, jnp.int32(1 << b)), jnp.int32(2)) for b in range(plan.bits)]
    other = [me + (1 - 2 * bit[b]) * (1 << b) for b in range(plan.bits)]
    return me, bit, other


def greet(plan, other):
    barrier = pltpu.get_barrier_semaphore()
    for b in range(plan.bits):
        pl.semaphore_signal(barrier, inc=1, device_id=(other[b],), device_id_type=MESH)
    pl.semaphore_wait(barrier, plan.bits)


class Gather:
    def __init__(self, plan, bit, other, send, recv):
        self.plan, self.bit, self.other, self.send, self.recv = plan, bit, other, send, recv

    def cols(self, part, mine):
        buf, src, stage, at, width = part["buf"], part["src"], part["stage"], part["at"], part["width"]
        if not part["split"]:
            return pl.ds(at, width)
        half = width // 2
        which = self.bit[0] if mine else 1 - self.bit[0]
        return pl.ds(pl.multiple_of(at + which * half, LANES), half)

    def copy(self, part, phase):
        plan, i = self.plan, part["i"]
        if phase == 0:
            cols = self.cols(part, False)
            src, dst, to = part["src"].at[:, cols], part["stage"], self.other[0]
        elif phase <= plan.chip_bits:
            order = plan.order(part["turn"])
            done, b = order[: phase - 1], order[phase - 1]
            idx = tuple(
                slice(None) if bb in done else self.bit[bb] for bb in range(plan.bits - 1, 0, -1)
            )
            ref = part["buf"].at[idx + (slice(None), self.cols(part, True))]
            src, dst, to = ref, ref, self.other[b]
        else:
            ref = part["buf"].at[(slice(None),) * (plan.chip_bits + 1) + (self.cols(part, True),)]
            src, dst, to = ref, ref, self.other[0]
        return pltpu.make_async_remote_copy(
            src_ref=src, dst_ref=dst, send_sem=self.send.at[i, phase], recv_sem=self.recv.at[i, phase],
            device_id=(to,), device_id_type=MESH,
        )

    def phases(self, part):
        return self.plan.chip_bits + (2 if part["split"] else 1)

    def start(self, part, phase):
        self.copy(part, phase).start()

    def wait(self, part, phase):
        self.copy(part, phase).wait()
        if phase == 0:
            cols = self.cols(part, True)
            own, got = part["src"][:, cols], part["stage"][...]
            lower = self.bit[0] == 0
            rows = jnp.concatenate([jnp.where(lower, own, got), jnp.where(lower, got, own)], 0)
            idx = tuple(self.bit[bb] for bb in range(self.plan.bits - 1, 0, -1))
            part["buf"][idx + (slice(None), cols)] = rows.astype(BF)

    def advance(self, part, phase):
        self.wait(part, phase)
        if phase + 1 < self.phases(part):
            self.start(part, phase + 1)


def gather_kernel(
    s_in, s_out, s_up, s_down, s_small, w_in, w_out, w_up, w_down, small,
    g0, g1, g2, g3, g4, g5, g6, send, recv, *, plan, width,
):
    me, bit, other = my_place(plan)
    greet(plan, other)
    gather = Gather(plan, bit, other, send, recv)
    make = lambda i, src, buf, stage, at, wide, split, turn: dict(
        i=i, src=src, buf=buf, stage=stage, at=at, width=wide, split=split, turn=turn
    )
    parts = [
        make(0, s_small, small, g6, 0, SMALL, False, 0),
        make(1, s_in, w_in, g0, 0, width, True, 0),
        make(2, s_in, w_in, g1, width, width, True, 1),
        make(3, s_in, w_in, g2, 2 * width, width, True, 2),
        make(4, s_out, w_out, g3, 0, width, True, 0),
        make(5, s_up, w_up, g4, 0, width, True, 1),
        make(6, s_down, w_down, g5, 0, width, True, 2),
    ]
    for part in parts:
        gather.start(part, 0)
    for phase in range(plan.chip_bits + 2):
        for part in parts:
            if phase < gather.phases(part):
                gather.advance(part, phase)


def gather_call(plan, shards, width):
    s_in, s_out, s_up, s_down, s_small = shards
    rows = s_in.shape[0]
    vm = pl.BlockSpec(memory_space=pltpu.VMEM)
    buf = lambda c: jax.ShapeDtypeStruct(plan.dims + (2 * rows, c), BF)
    stage = lambda c: pltpu.VMEM((rows, c), F32)
    got = pl.pallas_call(
        functools.partial(gather_kernel, plan=plan, width=width),
        in_specs=[vm] * 5,
        out_specs=[vm] * 5,
        out_shape=[buf(3 * width), buf(width), buf(width), buf(width), buf(SMALL)],
        scratch_shapes=[stage(width // 2)] * 6 + [stage(SMALL)]
        + [pltpu.SemaphoreType.DMA((7, plan.chip_bits + 2))] * 2,
        compiler_params=pltpu.CompilerParams(
            collective_id=0, has_side_effects=True, vmem_limit_bytes=VMEM_LIMIT
        ),
        name="gather",
    )(s_in, s_out, s_up, s_down, s_small)
    return [v.reshape(-1, v.shape[-1]) for v in got]


class Scatter:
    def __init__(self, plan, bit, other, send, recv):
        self.plan, self.bit, self.other, self.send, self.recv = plan, bit, other, send, recv

    def cols(self, part, mine):
        half = part["width"] // 2
        which = self.bit[0] if mine else 1 - self.bit[0]
        return pl.ds(pl.multiple_of(part["at"] + which * half, LANES), half)

    def order(self, part):
        return self.plan.order(part["turn"])[::-1]

    def index(self, part, phase, mine):
        done, b = self.order(part)[: phase - 1], self.order(part)[phase - 1]
        idx = []
        for bb in range(self.plan.bits - 1, 0, -1):
            if bb in done:
                continue
            idx.append((self.bit[b] if mine else 1 - self.bit[b]) if bb == b else slice(None))
        return tuple(idx)

    def rows(self, which):
        r = self.plan_rows
        return pl.ds(pl.multiple_of(which * r, 8), r)

    def copy(self, part, phase):
        plan, i = self.plan, part["i"]
        every = (slice(None),) * (plan.chip_bits + 1)
        if phase == 0:
            if part["split"]:
                src = part["src"].at[every + (self.cols(part, False),)]
            else:
                src = part["src"]
            dst, to = part["slots"][0], self.other[0]
        elif phase <= plan.chip_bits:
            src = part["slots"][phase - 1].at[self.index(part, phase, False)]
            dst, to = part["slots"][phase], self.other[self.order(part)[phase - 1]]
        else:
            r = part["sum"].shape[0] // 2
            src = part["sum"].at[pl.ds(pl.multiple_of((1 - self.bit[0]) * r, 8), r)]
            dst, to = part["last"], self.other[0]
        return pltpu.make_async_remote_copy(
            src_ref=src, dst_ref=dst, send_sem=self.send.at[i, phase], recv_sem=self.recv.at[i, phase],
            device_id=(to,), device_id_type=MESH,
        )

    def phases(self, part):
        return self.plan.chip_bits + (2 if part["split"] else 1)

    def start(self, part, phase):
        self.copy(part, phase).start()

    def wait(self, part, phase):
        plan = self.plan
        self.copy(part, phase).wait()
        every = (slice(None),) * (plan.chip_bits + 1)
        if phase > plan.chip_bits:
            return
        slot = part["slots"][phase]
        if phase == 0:
            if part["split"]:
                mine = part["src"][every + (self.cols(part, True),)]
            else:
                mine = part["src"][...]
        else:
            mine = part["slots"][phase - 1][self.index(part, phase, True)]
        total = mine.astype(F32) + slot[...].astype(F32)
        if phase == plan.chip_bits:
            part["sum"][...] = total
        else:
            slot[...] = total.astype(BF)

    def advance(self, part, phase):
        self.wait(part, phase)
        if phase + 1 < self.phases(part):
            self.start(part, phase + 1)

    def finish(self, part, out):
        r = part["sum"].shape[0] // 2
        own = part["sum"][pl.ds(pl.multiple_of(self.bit[0] * r, 8), r), :]
        if not part["split"]:
            out[...] = own
            return
        half = part["width"] // 2
        out[:, self.cols(part, True)] = own
        out[:, self.cols(part, False)] = part["last"][...]


def norm_exchange(plan, me, bit, squares, mine, boxes, send, recv):
    low = 1 << min(3, plan.bits)
    value = jnp.full((8, LANES), squares, F32)
    base = 0
    for span, stride in ((low, 1), (plan.count // low, low)):
        if span == 1:
            continue
        place = lax.rem(lax.div(me, jnp.int32(stride)), jnp.int32(span))
        mine[...] = value
        copies = []
        for d in range(1, span):
            to_place = lax.rem(place + d, jnp.int32(span))
            to = me + (to_place - place) * stride
            copies.append(pltpu.make_async_remote_copy(
                src_ref=mine, dst_ref=boxes.at[base + d - 1], send_sem=send.at[base + d - 1],
                recv_sem=recv.at[base + d - 1], device_id=(to,), device_id_type=MESH,
            ))
        for c in copies:
            c.start()
        for c in copies:
            c.wait()
        for d in range(1, span):
            value = value + boxes[base + d - 1]
        base += span - 1
    return value


def ring_partners(plan, me):
    low = 1 << min(3, plan.bits)
    found = []
    for span, stride in ((low, 1), (plan.count // low, low)):
        place = lax.rem(lax.div(me, jnp.int32(stride)), jnp.int32(span))
        for d in range(1, span):
            found.append(me + (lax.rem(place + d, jnp.int32(span)) - place) * stride)
    return found


def scatter_kernel(g_in, g_out, g_up, g_down, g_small, o_in, o_out, o_up, o_down, o_small, o_norm, *rest, plan, width):
    k = plan.chip_bits + 1
    slots = [rest[i * k : (i + 1) * k] for i in range(7)]
    rest = rest[7 * k :]
    sums, rest = rest[:7], rest[7:]
    lasts, rest = rest[:6], rest[6:]
    send, recv, mine, boxes, nsend, nrecv = rest
    me, bit, other = my_place(plan)
    barrier = pltpu.get_barrier_semaphore()
    partners = ring_partners(plan, me)
    for p in partners:
        pl.semaphore_signal(barrier, inc=1, device_id=(p,), device_id_type=MESH)
    pl.semaphore_wait(barrier, len(partners))
    scatter = Scatter(plan, bit, other, send, recv)
    parts = []
    for i, (src, at, wide, split, turn) in enumerate([
        (g_small, 0, SMALL, False, 0), (g_in, 0, width, True, 0), (g_in, width, width, True, 1), (g_in, 2 * width, width, True, 2),
        (g_out, 0, width, True, 0), (g_up, 0, width, True, 1), (g_down, 0, width, True, 2),
    ]):
        parts.append(dict(i=i, src=src, slots=slots[i], at=at, width=wide, split=split, turn=turn,
                          sum=sums[i], last=lasts[i - 1] if split else None))
    for part in parts:
        scatter.start(part, 0)
    for phase in range(plan.chip_bits + 2):
        for part in parts:
            if phase < scatter.phases(part):
                scatter.advance(part, phase)
    outs = [o_small, o_in, o_in, o_in, o_out, o_up, o_down]
    for part, out in zip(parts, outs):
        scatter.finish(part, out)
    total = sum(jnp.sum(o[...] * o[...]) for o in (o_small, o_in, o_out, o_up, o_down))
    o_norm[...] = jnp.sqrt(norm_exchange(plan, me, bit, total, mine, boxes, nsend, nrecv))


def scatter_call(plan, grads, width):
    g_in, g_out, g_up, g_down, g_small = grads
    rows = g_in.shape[0] // plan.count
    vm = pl.BlockSpec(memory_space=pltpu.VMEM)
    shaped = [g.reshape(plan.dims + (2 * rows, g.shape[-1])) for g in grads]
    slots = lambda c: [pltpu.VMEM(plan.dims[j:] + (2 * rows, c), BF) for j in range(plan.chip_bits + 1)]
    half = width // 2
    scratch = slots(SMALL)
    for _ in range(6):
        scratch += slots(half)
    scratch += [pltpu.VMEM((2 * rows, SMALL), F32)] + [pltpu.VMEM((2 * rows, half), F32)] * 6
    scratch += [pltpu.VMEM((rows, half), F32)] * 6
    scratch += [pltpu.SemaphoreType.DMA((7, plan.chip_bits + 2))] * 2
    low = 1 << min(3, plan.bits)
    boxes = low - 1 + plan.count // low - 1
    scratch += [pltpu.VMEM((8, LANES), F32), pltpu.VMEM((boxes, 8, LANES), F32)]
    scratch += [pltpu.SemaphoreType.DMA((boxes,))] * 2
    shard = lambda c: jax.ShapeDtypeStruct((rows, c), F32)
    return pl.pallas_call(
        functools.partial(scatter_kernel, plan=plan, width=width),
        in_specs=[vm] * 5,
        out_specs=[vm] * 6,
        out_shape=[shard(3 * width), shard(width), shard(width), shard(width), shard(SMALL),
                   jax.ShapeDtypeStruct((8, LANES), F32)],
        scratch_shapes=scratch,
        compiler_params=pltpu.CompilerParams(
            collective_id=1, has_side_effects=True, vmem_limit_bytes=VMEM_LIMIT
        ),
        name="scatter",
    )(*shaped)


def update_kernel(
    steps, rates, norm, g_in, g_out, g_up, g_down, g_small, *refs,
):
    states, outs, norm_o = refs[:18], refs[18:42], refs[42]
    norm_o[0, 0] = norm[0, 0]
    total = norm[0:1, 0:1]
    factor = jnp.minimum(1.0, CLIP_LIMIT / (total + NORM_EPS))
    t = jnp.full((1, 1), steps[0].astype(F32), F32)
    rate = rates[0]
    fix_one = 1.0 / (1.0 - jnp.exp(t * math.log(BETA_ONE)))
    fix_two = 1.0 / (1.0 - jnp.exp(t * math.log(BETA_TWO)))
    small = g_small[...]
    turned = jnp.concatenate([small, jnp.zeros((LANES - small.shape[0], SMALL), F32)], 0).T
    vec = turned[32:43, : small.shape[0]]
    vec = jnp.concatenate([vec[2:, :], vec[:2, :]], 0)
    grads = (g_in[...], g_out[...], g_up[...], g_down[...], small[:, :32], vec)
    for i, g in enumerate(grads):
        master, first, second = (states[3 * i + j][...] for j in range(3))
        g = g * factor
        first = BETA_ONE * first + (1.0 - BETA_ONE) * g
        second = BETA_TWO * second + (1.0 - BETA_TWO) * g * g
        change = first * fix_one / (jnp.sqrt(second * fix_two) + ADAM_EPS)
        if i < 5:
            change = change + DECAY_RATE * master
        for j, v in enumerate((g, first, second, master - rate * change)):
            outs[4 * i + j][...] = v


def update_call(step_count, learn_rate, norm, grads, states):
    vm, sm = pl.BlockSpec(memory_space=pltpu.VMEM), pl.BlockSpec(memory_space=pltpu.SMEM)
    shapes = [jax.ShapeDtypeStruct(states[3 * i].shape, F32) for i in range(6) for _ in range(4)]
    return pl.pallas_call(
        update_kernel,
        in_specs=[sm, sm] + [vm] * 24,
        out_specs=[vm] * 24 + [sm],
        out_shape=shapes + [jax.ShapeDtypeStruct((1, 1), F32)],
        compiler_params=pltpu.CompilerParams(vmem_limit_bytes=VMEM_LIMIT),
        name="update",
    )(step_count.reshape(1), learn_rate.reshape(1), norm, *grads, *states)


def body(
    count,
    tokens, eigvecs, counts, endpoints, cotangent,
    attend_in, attend_in_first, attend_in_second,
    attend_out, attend_out_first, attend_out_second,
    feed_up, feed_up_first, feed_up_second,
    feed_down, feed_down_first, feed_down_second,
    label_in, label_in_first, label_in_second,
    vectors, vectors_first, vectors_second,
    step_count, learn_rate,
):
    shard, width = feed_up.shape
    small_shard = jnp.concatenate(
        [label_in.T, vectors[9:].T, vectors[:9].T, jnp.zeros((shard, SMALL - 43), F32)], 1
    )
    shards = (attend_in, attend_out.T, feed_up, feed_down.T, small_shard)
    paired = Plan.fits(count, shard)
    if paired:
        plan = Plan(count)
        weights = gather_call(plan, shards, width)
    else:
        weights = [lax.all_gather(v.astype(BF), "dp", axis=0, tiled=True) for v in shards]
    out, tg, *grads = layer(
        tokens, jnp.swapaxes(eigvecs, 1, 2), counts.T, jnp.swapaxes(endpoints, 1, 2), cotangent, *weights, MOLS_STEP,
    )
    if paired:
        *sums, norm = scatter_call(plan, grads, width)
    else:
        sums = [lax.psum_scatter(v.astype(F32), "dp", scatter_dimension=0, tiled=True) for v in grads]
        squares = lax.psum(sum(jnp.sum(v * v) for v in sums), "dp")
        norm = jnp.full((8, LANES), jnp.sqrt(squares), F32)
    states = (
        attend_in, attend_in_first, attend_in_second,
        attend_out.T, attend_out_first.T, attend_out_second.T,
        feed_up, feed_up_first, feed_up_second,
        feed_down.T, feed_down_first.T, feed_down_second.T,
        label_in.T, label_in_first.T, label_in_second.T,
        vectors, vectors_first, vectors_second,
    )
    *new, norm = update_call(step_count, learn_rate, norm, sums, states)
    new = [v.T if i // 4 in (1, 3, 4) else v for i, v in enumerate(new)]
    return (out, tg, norm.reshape(()), *new)


MOLS_STEP = 2


def solution(mesh):
    rows, cols = P("dp", None), P(None, "dp")
    state = (rows,) * 3 + (cols,) * 3 + (rows,) * 3 + (cols,) * 9
    placed = (rows, P("dp", None, None), rows, P("dp", None, None), rows) + state + (P(), P())
    results = (rows,) * 4 + (cols,) * 4 + (rows,) * 4 + (cols,) * 12
    return jax.shard_map(
        functools.partial(body, mesh.shape["dp"]),
        mesh=mesh, in_specs=placed, out_specs=(rows, rows, P()) + results, check_vma=False,
    )
```

time: 1110 us -> 248 us (0.22)
  waiting for transfers between devices: 431 us -> 0 us
  Pallas kernels: 0 us -> 242 us
  local copies, waits for them, and re-layouts: 223 us -> 1.63 us
  matrix products: 187 us -> 0 us
  blocking collectives: 161 us -> 0 us
  other arithmetic: 81.6 us -> 1.38 us
  between operations: 22.1 us -> 2.15 us
    reduce_scatter x4 -> x0, waiting for transfers between devices: 430 us -> none  [the longest x1 122 us: body(): lax.psum_scatter(grad_in, 'dp', scatter_dimension=0, tiled=True)]
    pallas_call x0 -> x5, Pallas kernels: none -> 242 us  [the longest x1 74 us: layer(): pl.pallas_call(functools.partial(front_kernel, hd=hd, mols=mols_step, seq...]
    dot_general x42 -> x0, matrix products: 187 us -> none  [the longest x5 37.1 us: contract_rows(): lax.dot_general(left_side, right_side, (((0,), (0,)), ((), ())), preferre...]
    all_gather x2 -> x0, blocking collectives: 83.5 us -> none  [the longest x1 43.7 us: body(): lax.all_gather(copy_vectors, 'dp', axis=1, tiled=True)]
    gather x4 -> x0, local copies, waits for them, and re-layouts: 52.4 us -> none  [the longest x1 13.3 us: identifiers(): right_half = jnp.take_along_axis(eigvecs, target[:, :, None], 1)]
    reshape x8 -> x0, local copies, waits for them, and re-layouts: 48.6 us -> none  [the longest x4 24.6 us: to_heads(): return columns.reshape(blocks, block_mols, seq_len, HEADS, -1)]
    reduce_sum x18 -> x0, other arithmetic: 47.6 us -> none  [the longest x4 9.87 us: attend_block(): totals = jnp.sum(exponent, -1, keepdims=True)]
    psum x1 -> x0, blocking collectives: 40 us -> none  [body(): grad_norm = jnp.sqrt(lax.psum(local_squares, 'dp'))]
  transfers between devices with their start and end apart: 9 -> 0, of which waited for: 5 -> 0; matrix products, arithmetic and copies ran while one was open for 23% -> 0% of each run, Pallas kernels for 0% -> 0%
where the time goes in v1:
time: 248 us; the launch traced here: 247 us
  Pallas kernels  242 us (98%)
    pallas_call x1, Pallas kernels, layer(): pl.pallas_call(functools.partial(front_kernel, hd=hd, mols=mols_step, seq...  74 us
    pallas_call x1, Pallas kernels, layer(): pl.pallas_call(functools.partial(back_kernel, hd=hd, mols=mols_step, seq=...  60.9 us
    pallas_call x1, Pallas kernels, scatter_call(): pl.pallas_call(functools.partial(scatter_kernel, plan=plan, width=width),...  53.9 us
    pallas_call x1, Pallas kernels, gather_call(): pl.pallas_call(functools.partial(gather_kernel, plan=plan, width=width),...  50 us

profile of v1, /device:TPU:0, one launch (start us, length us, event | category | flops | bytes accessed | tf_op | source)
XLA Modules:
  0.0 247.1 jit_solution(7184367732606346358)
XLA Ops:
  0.7 0.7 slice.6
  1.4 0.1 copy.54
  1.4 0.8 copy.55
  2.2 0.1 pad.3.clone
  2.3 1.4 maximum_maximum_fusion.s_small
  3.7 50.0 %gather.1 = (bf16[2,2,2,2,48,2304]{5,4,3,2,1,0:T(8,128)(2,1)}, bf16[2,2,2,2,48,768]{5,4,3,2,1,0:T(8,128)(2,1)}, bf16[2,2,2,2,48,768]{5,4,3,2,1,0:T(8,128)(2,1)},...) custom-call(f32[24,2304]{1,0:T(8,128)} %refs_0_.1, f32[24,768]{1,0:T(8,128)} %bitcast.53, ...), custom_call_target="tpu_custom_call" | custom-call | tf_op jit(solution)/shard_map/gather/pallas_call | solution.py:532
  53.7 74.0 %front.1 = (bf16[2048,768]{1,0:T(8,128)(2,1)}, bf16[2048,2304]{1,0:T(8,128)(2,1)}, f32[16,16,256]{2,1,0:T(8,128)}, f32[2048,768]{1,0:T(8,128)}, f32[2048,768]{1,...) custom-call(s32[2,16]{1,0:T(2,128)} %bitcast.71, ...), custom_call_target="tpu_custom_call" | custom-call | tf_op jit(solution)/shard_map/front/pallas_call | solution.py:348
  127.7 60.9 %back.1 = (f32[2048,768]{1,0:T(8,128)}, bf16[768,2304]{1,0:T(8,128)(2,1)}, bf16[768,128]{1,0:T(8,128)(2,1)}) custom-call(s32[2,16]{1,0:T(2,128)} %bitcast.72, bf16[2048,2304]{1,0:T(8,128)(2,1)} %get-tuple-element.83.proj, f32[16,16,256]{2,1,0:T(8,128)} %get-tuple-element.84.lse, f32[2048,768]{1,0:T(8,128)} %get-tuple-element.85.emb, ...), custom_call_target="tpu_custom_call" | custom-call | tf_op jit(solution)/shard_map/back/pallas_call | solution.py:382
  188.6 53.9 %scatter.1 = (f32[24,2304]{1,0:T(8,128)}, f32[24,768]{1,0:T(8,128)}, f32[24,768]{1,0:T(8,128)}, f32[24,768]{1,0:T(8,128)}, f32[24,128]{1,0:T(8,128)}, /*index=5*/f32[8,128]{1,0:T(8,128)}) custom-call(bf16[2,2,2,2,48,2304]{5,4,3,2,1,0:T(8,128)(2,1)} %bitcast.44, bf16[2,2,2,2,48,768]{5,4,3,2,1,0:T(8,128)(2,1)} %bitcast.45, ...), custom_call_target="tpu_custom_call" | custom-call | tf_op jit(solution)/shard_map/scatter/pallas_call | solution.py:724
  243.8 3.1 %update.1 = (f32[24,2304]{1,0:T(8,128)}, f32[24,2304]{1,0:T(8,128)}, f32[24,2304]{1,0:T(8,128)}, f32[24,2304]{1,0:T(8,128)}, f32[24,768]{1,0:T(8,128)}, /*index=...) custom-call(s32[1]{0:T(128)} %bitcast.40.steps, ...), custom_call_target="tpu_custom_call" | custom-call | tf_op jit(solution)/shard_map/update/pallas_call | solution.py:769
  (1 shorter events, 0.0 us)

commit v2 on v1

v2 whole, which is shorter than its diff:
```python
import functools
import math

import jax
import jax.numpy as jnp
from jax import lax
from jax.experimental import pallas as pl
from jax.experimental.pallas import tpu as pltpu
from jax.sharding import PartitionSpec as P

HEADS = 32
EPS_NORM = 1e-05
MASK_FILL = -1e30
SQRT_HALF = 0.7071067811865476
INV_SQRT_TWO_PI = 0.3989422804014327
BETA_ONE = 0.9
BETA_TWO = 0.999
ADAM_EPS = 1e-08
DECAY_RATE = 0.01
CLIP_LIMIT = 1.0
NORM_EPS = 1e-06
LOG2E = 1.4426950408889634

BF = jnp.bfloat16
F32 = jnp.float32
MESH = pl.DeviceIdType.MESH
LANES = 128
VMEM_LIMIT = 60 << 20

SMALL = 128
NODE, EDGE = 32, 33
GAIN1, SHIFT1, QBIAS, VBIAS, OBIAS, GAIN2, SHIFT2, UBIAS, DBIAS = range(34, 43)


def nn(a, b):
    return lax.dot_general(a, b, (((1,), (0,)), ((), ())), preferred_element_type=F32)


def nt(a, b):
    return lax.dot_general(a, b, (((1,), (1,)), ((), ())), preferred_element_type=F32)


def tn(a, b):
    return lax.dot_general(a, b, (((0,), (0,)), ((), ())), preferred_element_type=F32)


def layer_stats(values):
    centred = values - jnp.mean(values, -1, keepdims=True)
    recip_std = lax.rsqrt(jnp.mean(centred * centred, -1, keepdims=True) + EPS_NORM)
    return centred * recip_std, recip_std


def norm_back(grad_out, normed, recip_std, gain_row):
    scaled = grad_out * gain_row
    return recip_std * (
        scaled
        - jnp.mean(scaled, -1, keepdims=True)
        - normed * jnp.mean(scaled * normed, -1, keepdims=True)
    )


class Heads:
    def __init__(self, width):
        self.dim = width // HEADS
        span = 1
        while (span * self.dim) % LANES:
            span *= 2
        self.block = span
        self.tiles = span * self.dim // LANES
        self.blocks = HEADS // span

    def first(self, head):
        return head * self.dim // LANES

    def last(self, head):
        return ((head + 1) * self.dim - 1) // LANES

    def heads_of(self, tile):
        return [h for h in range(self.block) if self.first(h) <= tile <= self.last(h)]

    def slot(self, tile, head):
        return sum(len(self.heads_of(t)) for t in range(tile)) + head - self.heads_of(tile)[0]

    def slots(self):
        return sum(len(self.heads_of(t)) for t in range(self.tiles))

    def mask(self, tile, head):
        lane = lax.broadcasted_iota(jnp.int32, (1, LANES), 1) + tile * LANES
        inside = jnp.logical_and(lane >= head * self.dim, lane < (head + 1) * self.dim)
        return inside.astype(F32).astype(BF)


def masked(value, mask):
    rows = value.shape[0]
    return (value.reshape(rows // 16, 16, LANES) * mask[None]).reshape(rows, LANES)


def set_masks(hd, masks):
    for t in range(hd.tiles):
        for h in hd.heads_of(t):
            masks[hd.slot(t, h)] = jnp.broadcast_to(hd.mask(t, h), (16, LANES))


def across(parts):
    return parts[0] if len(parts) == 1 else jnp.concatenate(parts, 1)


def pair_rows(hd, masks, tiles_of, pair):
    h0, h1 = 2 * pair, 2 * pair + 1
    lo, hi = hd.first(h0), hd.last(h1)
    rows = []
    for h in (h0, h1):
        parts = []
        for t in range(lo, hi + 1):
            if hd.first(h) <= t <= hd.last(h):
                parts.append(masked(tiles_of[t], masks[hd.slot(t, h)]))
            else:
                parts.append(jnp.zeros_like(tiles_of[t]))
        rows.append(across(parts))
    return jnp.concatenate(rows, 0)


def pair_full(hd, tiles_of, pair):
    return across([tiles_of[t] for t in range(hd.first(2 * pair), hd.last(2 * pair + 1) + 1)])


def tile_rows(hd, masks, tile_value, tile):
    return jnp.concatenate([masked(tile_value, masks[hd.slot(tile, h)]) for h in hd.heads_of(tile)], 0)


class Plan:
    def __init__(self, count):
        self.count = count
        self.bits = count.bit_length() - 1
        self.chip_bits = self.bits - 1
        self.dims = (2,) * self.chip_bits
        near = list(range(1, min(4, self.bits)))
        self.far = list(range(self.bits - 1, near[-1], -1))
        self.turns = [near[i:] + near[:i] for i in range(len(near))]

    def order(self, part):
        return self.far + self.turns[part % len(self.turns)]

    @staticmethod
    def fits(count, rows):
        return count >= 16 and count & (count - 1) == 0 and rows % 8 == 0


def my_place(plan):
    me = lax.axis_index("dp")
    bit = [lax.rem(lax.div(me, jnp.int32(1 << b)), jnp.int32(2)) for b in range(plan.bits)]
    other = [me + (1 - 2 * bit[b]) * (1 << b) for b in range(plan.bits)]
    return me, bit, other


def greet(plan, other):
    barrier = pltpu.get_barrier_semaphore()
    for b in range(plan.bits):
        pl.semaphore_signal(barrier, inc=1, device_id=(other[b],), device_id_type=MESH)
    pl.semaphore_wait(barrier, plan.bits)


class Gather:
    def __init__(self, plan, bit, other, send, recv):
        self.plan, self.bit, self.other, self.send, self.recv = plan, bit, other, send, recv

    def cols(self, part, mine):
        buf, src, stage, at, width = part["buf"], part["src"], part["stage"], part["at"], part["width"]
        if not part["split"]:
            return pl.ds(at, width)
        half = width // 2
        which = self.bit[0] if mine else 1 - self.bit[0]
        return pl.ds(pl.multiple_of(at + which * half, LANES), half)

    def copy(self, part, phase):
        plan, i = self.plan, part["i"]
        if phase == 0:
            cols = self.cols(part, False)
            src, dst, to = part["src"].at[:, cols], part["stage"], self.other[0]
        elif phase <= plan.chip_bits:
            order = plan.order(part["turn"])
            done, b = order[: phase - 1], order[phase - 1]
            idx = tuple(
                slice(None) if bb in done else self.bit[bb] for bb in range(plan.bits - 1, 0, -1)
            )
            ref = part["buf"].at[idx + (slice(None), self.cols(part, True))]
            src, dst, to = ref, ref, self.other[b]
        else:
            ref = part["buf"].at[(slice(None),) * (plan.chip_bits + 1) + (self.cols(part, True),)]
            src, dst, to = ref, ref, self.other[0]
        return pltpu.make_async_remote_copy(
            src_ref=src, dst_ref=dst, send_sem=self.send.at[i, phase], recv_sem=self.recv.at[i, phase],
            device_id=(to,), device_id_type=MESH,
        )

    def phases(self, part):
        return self.plan.chip_bits + (2 if part["split"] else 1)

    def start(self, part, phase):
        self.copy(part, phase).start()

    def wait(self, part, phase):
        self.copy(part, phase).wait()
        if phase == 0:
            cols = self.cols(part, True)
            own, got = part["src"][:, cols], part["stage"][...]
            lower = self.bit[0] == 0
            rows = jnp.concatenate([jnp.where(lower, own, got), jnp.where(lower, got, own)], 0)
            idx = tuple(self.bit[bb] for bb in range(self.plan.bits - 1, 0, -1))
            part["buf"][idx + (slice(None), cols)] = rows.astype(BF)

    def advance(self, part, phase):
        self.wait(part, phase)
        if phase + 1 < self.phases(part):
            self.start(part, phase + 1)


class Scatter:
    def __init__(self, plan, bit, other, send, recv):
        self.plan, self.bit, self.other, self.send, self.recv = plan, bit, other, send, recv

    def cols(self, part, mine):
        half = part["width"] // 2
        which = self.bit[0] if mine else 1 - self.bit[0]
        return pl.ds(pl.multiple_of(part["at"] + which * half, LANES), half)

    def order(self, part):
        return self.plan.order(part["turn"])[::-1]

    def index(self, part, phase, mine):
        done, b = self.order(part)[: phase - 1], self.order(part)[phase - 1]
        idx = []
        for bb in range(self.plan.bits - 1, 0, -1):
            if bb in done:
                continue
            idx.append((self.bit[b] if mine else 1 - self.bit[b]) if bb == b else slice(None))
        return tuple(idx)

    def rows(self, which):
        r = self.plan_rows
        return pl.ds(pl.multiple_of(which * r, 8), r)

    def copy(self, part, phase):
        plan, i = self.plan, part["i"]
        every = (slice(None),) * (plan.chip_bits + 1)
        if phase == 0:
            if part["split"]:
                src = part["src"].at[every + (self.cols(part, False),)]
            else:
                src = part["src"]
            dst, to = part["slots"][0], self.other[0]
        elif phase <= plan.chip_bits:
            src = part["slots"][phase - 1].at[self.index(part, phase, False)]
            dst, to = part["slots"][phase], self.other[self.order(part)[phase - 1]]
        else:
            r = part["sum"].shape[0] // 2
            src = part["sum"].at[pl.ds(pl.multiple_of((1 - self.bit[0]) * r, 8), r)]
            dst, to = part["last"], self.other[0]
        return pltpu.make_async_remote_copy(
            src_ref=src, dst_ref=dst, send_sem=self.send.at[i, phase], recv_sem=self.recv.at[i, phase],
            device_id=(to,), device_id_type=MESH,
        )

    def phases(self, part):
        return self.plan.chip_bits + (2 if part["split"] else 1)

    def start(self, part, phase):
        self.copy(part, phase).start()

    def wait(self, part, phase):
        plan = self.plan
        self.copy(part, phase).wait()
        every = (slice(None),) * (plan.chip_bits + 1)
        if phase > plan.chip_bits:
            return
        slot = part["slots"][phase]
        if phase == 0:
            if part["split"]:
                mine = part["src"][every + (self.cols(part, True),)]
            else:
                mine = part["src"][...]
        else:
            mine = part["slots"][phase - 1][self.index(part, phase, True)]
        total = mine.astype(F32) + slot[...].astype(F32)
        if phase == plan.chip_bits:
            part["sum"][...] = total
        else:
            slot[...] = total.astype(BF)

    def advance(self, part, phase):
        self.wait(part, phase)
        if phase + 1 < self.phases(part):
            self.start(part, phase + 1)

    def finish(self, part, out):
        r = part["sum"].shape[0] // 2
        own = part["sum"][pl.ds(pl.multiple_of(self.bit[0] * r, 8), r), :]
        if not part["split"]:
            out[...] = own
            return
        half = part["width"] // 2
        out[:, self.cols(part, True)] = own
        out[:, self.cols(part, False)] = part["last"][...]


def norm_exchange(plan, me, bit, squares, mine, boxes, send, recv):
    low = 1 << min(3, plan.bits)
    value = jnp.full((8, LANES), squares, F32)
    base = 0
    for span, stride in ((low, 1), (plan.count // low, low)):
        if span == 1:
            continue
        place = lax.rem(lax.div(me, jnp.int32(stride)), jnp.int32(span))
        mine[...] = value
        copies = []
        for d in range(1, span):
            to_place = lax.rem(place + d, jnp.int32(span))
            to = me + (to_place - place) * stride
            copies.append(pltpu.make_async_remote_copy(
                src_ref=mine, dst_ref=boxes.at[base + d - 1], send_sem=send.at[base + d - 1],
                recv_sem=recv.at[base + d - 1], device_id=(to,), device_id_type=MESH,
            ))
        for c in copies:
            c.start()
        for c in copies:
            c.wait()
        for d in range(1, span):
            value = value + boxes[base + d - 1]
        base += span - 1
    return value


def ring_partners(plan, me):
    low = 1 << min(3, plan.bits)
    found = []
    for span, stride in ((low, 1), (plan.count // low, low)):
        place = lax.rem(lax.div(me, jnp.int32(stride)), jnp.int32(span))
        for d in range(1, span):
            found.append(me + (lax.rem(place + d, jnp.int32(span)) - place) * stride)
    return found


def mat(ref, *cols):
    value = ref[(slice(None),) * (len(ref.shape) - 1) + cols] if cols else ref[...]
    return value.reshape(-1, value.shape[-1])


def front_kernel(*refs, plan, hd, mols, wide, seq, steps, steps2):
    refs = list(refs)
    take = lambda k: [refs.pop(0) for _ in range(k)]
    counts, tokens, eig, ends, cot = take(5)
    shards = take(5)
    out_o, proj_o, lse_o, dmid_o, dmix_o, labt_o, gout_o, gup_o, gdown_o, gvec_o, smallt_o, emb_o, inp_o, win_o = take(14)
    w_in, w_out, w_up, w_down, small = take(5)
    stages = take(7)
    small_t, masks, tok_s, emb_s, inp_s, mixed_s, p_buf, acc_out, acc_up, acc_down, acc_vec = take(11)
    send, recv, keep = take(3)
    s_in, s_out, s_up, s_down, s_small = shards
    step = pl.program_id(0)
    width = w_out.shape[-1]
    across_tiles = width // LANES
    score = hd.dim ** -0.5
    rows_all = mols * seq
    me, bit, other = my_place(plan)
    gather = Gather(plan, bit, other, send, recv)
    make = lambda i, src, buf, at, wide, split, t: dict(
        i=i, src=src, buf=buf, stage=stages[i], at=at, width=wide, split=split, turn=t
    )
    early = [
        make(0, s_small, small, 0, SMALL, False, 0),
        make(1, s_in, w_in, 0, width, True, 0),
        make(2, s_in, w_in, width, width, True, 1),
        make(3, s_in, w_in, 2 * width, width, True, 2),
    ]
    late = [
        make(4, s_out, w_out, 0, width, True, 0),
        make(5, s_up, w_up, 0, width, True, 1),
        make(6, s_down, w_down, 0, width, True, 2),
    ]
    final = plan.chip_bits + 1
    kept = [pltpu.make_async_copy(a, b, keep.at[i]) for i, (a, b) in enumerate(((w_in, win_o), (emb_s, emb_o), (inp_s, inp_o)))]
    get_tokens = pltpu.make_async_copy(tokens, tok_s, keep.at[3])

    row = lambda i: small_t[i : i + 1, :]

    def embed(group, carry):
        iota0 = lax.broadcasted_iota(jnp.int32, (seq, seq), 0)
        iota1 = lax.broadcasted_iota(jnp.int32, (seq, seq), 1)
        token_row = lax.broadcasted_iota(jnp.int32, (1, seq), 1)
        kind_row = lax.broadcasted_iota(jnp.int32, (16, seq), 0)
        one = lambda c: c.astype(F32).astype(BF)
        label_rows = []
        for g in range(mols):
            m = group * mols + g
            nodes = counts[0, m]
            live = nodes + counts[1, m]
            eig_f = eig[m]
            shift = one(jnp.logical_and(iota1 - iota0 == nodes, iota1 < live))
            picks = jnp.concatenate([one(iota0 == ends[m, end : end + 1, :]) for end in range(2)], 1)
            edge_lab = nn(eig_f.astype(BF), picks).astype(BF)
            moved = nn(jnp.concatenate([edge_lab[:, :seq], edge_lab[:, seq:]], 0), shift)
            at_node = token_row < nodes
            is_node = at_node.astype(F32)
            is_edge = jnp.logical_and(token_row >= nodes, token_row < live).astype(F32)
            kind = jnp.where(kind_row == 0, is_node, jnp.where(kind_row == 1, is_edge, 0.0))
            lab = jnp.concatenate(
                [jnp.where(at_node, eig_f, moved[:16]), jnp.where(at_node, eig_f, moved[16:]), kind], 0
            )
            labt_o[m] = lab.astype(BF)
            pad = jnp.zeros((SMALL - lab.shape[0], seq), F32)
            label_rows.append(jnp.concatenate([lab, pad], 0).T.astype(BF))
        labels = jnp.concatenate(label_rows, 0)
        here = pl.ds(pl.multiple_of(group * rows_all, rows_all), rows_all)
        embedded = tok_s[here, :].astype(F32) + nn(labels, small_t[...].astype(BF))
        emb_s[here, :] = embedded
        normed, _ = layer_stats(embedded)
        value = (normed * row(GAIN1) + row(SHIFT1)).astype(BF)
        for t in range(across_tiles):
            inp_s[t, here, :] = value[:, t * LANES : (t + 1) * LANES]
        return carry

    @pl.when(step == 0)
    def _():
        get_tokens.start()
        greet(plan, other)
        for part in early + late:
            gather.start(part, 0)
        set_masks(hd, masks)
        acc_out[...] = jnp.zeros_like(acc_out)
        acc_up[...] = jnp.zeros_like(acc_up)
        acc_down[...] = jnp.zeros_like(acc_down)
        acc_vec[...] = jnp.zeros_like(acc_vec)
        for phase in range(final):
            for part in early:
                if part["split"] and phase == final - 1:
                    continue
                gather.advance(part, phase)
        small_t[...] = mat(small).astype(F32).T
        smallt_o[...] = small_t[...]
        get_tokens.wait()
        cut = (steps + 1) // 2
        lax.fori_loop(0, cut, embed, 0)
        for part in early[1:]:
            gather.advance(part, final - 1)
        lax.fori_loop(cut, steps, embed, 0)
        for part in early[1:]:
            gather.advance(part, final)
        for part in late:
            gather.advance(part, 0)
        for copy in kept:
            copy.start()

    @pl.when(step < steps)
    def _():
        here = pl.ds(pl.multiple_of(step * rows_all, rows_all), rows_all)
        input_one = across([inp_s[t, here, :] for t in range(across_tiles)])
        for part in range(3):
            value = nn(input_one, mat(w_in, slice(part * width, (part + 1) * width)))
            if part == 0:
                value = value + row(QBIAS)
            if part == 2:
                value = value + row(VBIAS)
            value = value.astype(BF)
            for t in range(across_tiles):
                proj_o[part * across_tiles + t] = value[:, t * LANES : (t + 1) * LANES]

        for m in range(mols):
            nodes = counts[0, step * mols + m]
            live = nodes + counts[1, step * mols + m]
            key_live = lax.broadcasted_iota(jnp.int32, (seq, 2 * seq), 0) < live
            rows = slice(m * seq, (m + 1) * seq)
            for b in range(hd.blocks):
                get = lambda part: [proj_o[part * across_tiles + b * hd.tiles + t, rows, :] for t in range(hd.tiles)]
                q, k, v = get(0), get(1), get(2)
                for pair in range(hd.block // 2):
                    scores = nt(pair_full(hd, k, pair), pair_rows(hd, masks, q, pair))
                    scores = jnp.where(key_live, scores, MASK_FILL)
                    top = jnp.max(scores, 0, keepdims=True)
                    ex = jnp.exp2((scores - top) * (score * LOG2E))
                    total = jnp.sum(ex, 0, keepdims=True)
                    shares = (ex * (1.0 / total)).astype(BF)
                    at = b * (hd.block // 2) + pair
                    lse_o[m, at : at + 1, :] = top + jnp.log2(total) * (1.0 / (score * LOG2E))
                    for i in range(2):
                        p_buf[b * hd.block + 2 * pair + i] = shares[:, i * seq : (i + 1) * seq].T
                for t in range(hd.tiles):
                    hs = hd.heads_of(t)
                    mixed = nn(across([p_buf[b * hd.block + h] for h in hs]), tile_rows(hd, masks, v[t], t))
                    put = pl.ds(pl.multiple_of(step * rows_all + m * seq, seq), seq)
                    mixed_s[b * hd.tiles + t, put, :] = mixed.astype(BF)

    for phase in range(1, final + 1):
        @pl.when(step == min((1, 2, 4, 6)[min(phase, 4) - 1] + max(phase - 4, 0), steps - 1))
        def _():
            for part in late:
                gather.advance(part, phase)

    @pl.when(step >= steps)
    def _():
        here = pl.ds(pl.multiple_of((step - steps) * wide, wide), wide)
        mixed = across([mixed_s[t, here, :] for t in range(across_tiles)])
        middle = emb_s[here, :] + (nt(mixed, mat(w_out)) + row(OBIAS))
        normed2, recip2 = layer_stats(middle)
        input_two = (normed2 * row(GAIN2) + row(SHIFT2)).astype(BF)
        pre = nn(input_two, mat(w_up)) + row(UBIAS)
        half_erf = 0.5 * (1.0 + lax.erf(pre * SQRT_HALF))
        act = (pre * half_erf).astype(BF)
        slope = half_erf + pre * jnp.exp(-0.5 * pre * pre) * INV_SQRT_TWO_PI
        out_o[...] = (middle + (nt(act, mat(w_down)) + row(DBIAS))).astype(BF)
        back = cot[...]
        back_f = back.astype(F32)
        d_pre = (nn(back, mat(w_down)) * slope).astype(BF)
        acc_down[...] += tn(back, act)
        acc_up[...] += tn(input_two, d_pre)
        d_in2 = nt(d_pre, mat(w_up))
        d_mid = back_f + norm_back(d_in2, normed2, recip2, row(GAIN2))
        dmid_o[...] = d_mid
        branch = d_mid.astype(BF)
        acc_out[...] += tn(branch, mixed)
        d_mixed = nn(branch, mat(w_out)).astype(BF)
        for t in range(across_tiles):
            dmix_o[t] = d_mixed[:, t * LANES : (t + 1) * LANES]
        add = lambda v: jnp.sum(v, 0, keepdims=True)
        sums = {
            OBIAS: add(branch.astype(F32)),
            GAIN2: add(d_in2 * normed2),
            SHIFT2: add(d_in2),
            UBIAS: add(d_pre.astype(F32)),
            DBIAS: add(back_f),
        }
        for i, v in sums.items():
            acc_vec[i - 34 : i - 33, :] += v

    @pl.when(step == steps + steps2 - 1)
    def _():
        for acc, out in ((acc_out, gout_o), (acc_up, gup_o), (acc_down, gdown_o)):
            out[...] = acc[...].astype(BF)
        gvec_o[...] = acc_vec[...]
        for copy in kept:
            copy.wait()


class ShareSmall:
    def __init__(self, plan, me, src, boxes, part, boxes2, send, recv):
        self.src, self.boxes, self.part, self.boxes2 = src, boxes, part, boxes2
        low = src.shape[1]
        high = plan.count // low
        self.place, self.level = lax.rem(me, jnp.int32(low)), lax.div(me, jnp.int32(low))
        self.one, self.two = [], []
        for d in range(1, low):
            to = lax.rem(self.place + d, jnp.int32(low))
            self.one.append(pltpu.make_async_remote_copy(
                src_ref=src.at[:, to], dst_ref=boxes.at[d - 1], send_sem=send.at[d - 1], recv_sem=recv.at[d - 1],
                device_id=(me + to - self.place,), device_id_type=MESH,
            ))
        for d in range(1, high):
            to = lax.rem(self.level + d, jnp.int32(high))
            at = low - 2 + d
            self.two.append(pltpu.make_async_remote_copy(
                src_ref=part.at[to], dst_ref=boxes2.at[d - 1], send_sem=send.at[at], recv_sem=recv.at[at],
                device_id=(me + (to - self.level) * low,), device_id_type=MESH,
            ))

    def begin(self):
        for c in self.one:
            c.start()

    def middle(self):
        total = self.src[:, self.place]
        for d, c in enumerate(self.one):
            c.wait()
            total = total + self.boxes[d]
        self.part[...] = total
        for c in self.two:
            c.start()

    def end(self):
        total = self.part[self.level]
        for d, c in enumerate(self.two):
            c.wait()
            total = total + self.boxes2[d]
        return total


def back_kernel(*refs, plan, hd, mols, wide, seq, steps, steps2):
    refs = list(refs)
    take = lambda k: [refs.pop(0) for _ in range(k)]
    counts, proj, lse, inp, emb, dmid, dmix, labt, w_in, small_t, gvec, g_out, g_up, g_down = take(14)
    tg_o, o_in, o_out, o_up, o_down, o_small, o_norm = take(7)
    masks, pt_buf, dst_buf, ds_buf, dproj_s, acc_in, g_in, acc_vec, acc_lab = take(9)
    k = plan.chip_bits + 1
    slots = [take(k) for _ in range(6)]
    part_sums, lasts = take(6), take(6)
    send, recv = take(2)
    small_s, small_box, small_part, small_box2, ssend, srecv = take(6)
    mine, boxes, nsend, nrecv = take(4)
    step = pl.program_id(0)
    width = g_out.shape[-1]
    across_tiles = width // LANES
    score = hd.dim ** -0.5
    rows_all = mols * seq
    me, bit, other = my_place(plan)
    scatter = Scatter(plan, bit, other, send, recv)
    parts = []
    for i, (src, at, t) in enumerate([
        (g_in, 0, 0), (g_in, width, 1), (g_in, 2 * width, 2), (g_out, 0, 0), (g_up, 0, 1), (g_down, 0, 2),
    ]):
        parts.append(dict(i=i, src=src, slots=slots[i], at=at, width=width, split=True, turn=t,
                          sum=part_sums[i], last=lasts[i]))
    late, early = parts[:3], parts[3:]
    final = plan.chip_bits + 1

    @pl.when(step == 0)
    def _():
        barrier = pltpu.get_barrier_semaphore()
        partners = ring_partners(plan, me)
        for p in partners:
            pl.semaphore_signal(barrier, inc=1, device_id=(p,), device_id_type=MESH)
        pl.semaphore_wait(barrier, len(partners))
        for part in early:
            scatter.start(part, 0)
        set_masks(hd, masks)
        acc_in[...] = jnp.zeros_like(acc_in)
        acc_vec[...] = gvec[...]
        acc_lab[...] = jnp.zeros_like(acc_lab)

    row = lambda i: small_t[i : i + 1, :]

    @pl.when(step < steps)
    def _():
        here = pl.ds(pl.multiple_of(step * rows_all, rows_all), rows_all)
        for m in range(mols):
            nodes = counts[0, step * mols + m]
            live = nodes + counts[1, step * mols + m]
            key_live = lax.broadcasted_iota(jnp.int32, (seq, 2 * seq), 0) < live
            rows = slice(m * seq, (m + 1) * seq)
            put = pl.ds(pl.multiple_of(step * rows_all + m * seq, seq), seq)
            for b in range(hd.blocks):
                get = lambda ref, part: [ref[part * across_tiles + b * hd.tiles + t, rows, :] for t in range(hd.tiles)]
                q, k, v, do = get(proj, 0), get(proj, 1), get(proj, 2), get(dmix, 0)
                for pair in range(hd.block // 2):
                    scores = nt(pair_full(hd, k, pair), pair_rows(hd, masks, q, pair))
                    scores = jnp.where(key_live, scores, MASK_FILL)
                    at = b * (hd.block // 2) + pair
                    p = jnp.exp2((scores - lse[m, at : at + 1, :]) * (score * LOG2E))
                    dp = nt(pair_full(hd, v, pair), pair_rows(hd, masks, do, pair))
                    inner = jnp.sum(p * dp, 0, keepdims=True)
                    ds = (p * (dp - inner)).astype(BF)
                    p = p.astype(BF)
                    for i in range(2):
                        h = b * hd.block + 2 * pair + i
                        pt_buf[h] = p[:, i * seq : (i + 1) * seq]
                        dst_buf[h] = ds[:, i * seq : (i + 1) * seq]
                        ds_buf[h] = ds[:, i * seq : (i + 1) * seq].T
                for t in range(hd.tiles):
                    hs = [b * hd.block + h for h in hd.heads_of(t)]
                    at = b * hd.tiles + t
                    d_v = nn(across([pt_buf[h] for h in hs]), tile_rows(hd, masks, do[t], t))
                    d_k = nn(across([dst_buf[h] for h in hs]), tile_rows(hd, masks, q[t], t)) * score
                    d_q = nn(across([ds_buf[h] for h in hs]), tile_rows(hd, masks, k[t], t)) * score
                    dproj_s[at, put, :] = d_q.astype(BF)
                    dproj_s[across_tiles + at, put, :] = d_k.astype(BF)
                    dproj_s[2 * across_tiles + at, put, :] = d_v.astype(BF)
        input_one = across([inp[t] for t in range(across_tiles)])
        d_proj = across([dproj_s[t, here, :] for t in range(3 * across_tiles)])
        acc_in[...] += tn(input_one, d_proj)
        add = lambda v: jnp.sum(v, 0, keepdims=True)
        acc_vec[QBIAS - 34 : QBIAS - 33, :] += add(d_proj[:, :width].astype(F32))
        acc_vec[VBIAS - 34 : VBIAS - 33, :] += add(d_proj[:, 2 * width :].astype(F32))

    for phase in range(final + 1):
        @pl.when(step == min((0, 2, 3, 4)[min(phase, 3)] + 2 * max(phase - 3, 0), steps - 1))
        def _():
            for part in early:
                scatter.advance(part, phase)

    @pl.when(step == steps - 1)
    def _():
        for part in late:
            cols = slice(part["at"], part["at"] + width)
            g_in[(slice(None),) * (plan.chip_bits + 1) + (cols,)] = acc_in[:, cols].astype(BF).reshape(
                g_in.shape[:-1] + (width,)
            )
            scatter.start(part, 0)

    @pl.when(step >= steps)
    def _():
        here = pl.ds(pl.multiple_of((step - steps) * wide, wide), wide)
        normed, recip = layer_stats(emb[...])
        d_proj = across([dproj_s[t, here, :] for t in range(3 * across_tiles)])
        d_in1 = nt(d_proj, mat(w_in))
        tg = dmid[...] + norm_back(d_in1, normed, recip, row(GAIN1))
        tg_o[...] = tg
        tg_hi = tg.astype(BF)
        tg_lo = (tg - tg_hi.astype(F32)).astype(BF)
        lab = jnp.concatenate([labt[m] for m in range(wide // seq)], 1)
        acc_lab[...] += nn(lab, tg_hi)
        acc_lab[32:48, :] += nn(lab[32:48, :], tg_lo)
        add = lambda v: jnp.sum(v, 0, keepdims=True)
        acc_vec[GAIN1 - 34 : GAIN1 - 33, :] += add(d_in1 * normed)
        acc_vec[SHIFT1 - 34 : SHIFT1 - 33, :] += add(d_in1)

    for phase in range(min(final, steps2 - 1)):
        @pl.when(step == steps + phase)
        def _():
            for part in late:
                scatter.advance(part, phase)

    @pl.when(step == steps + steps2 - 1)
    def _():
        full = jnp.concatenate(
            [acc_lab[0:32, :], acc_lab[32:34, :], acc_vec[0:9, :], jnp.zeros((SMALL - 43, width), F32)], 0
        )
        small_s[...] = full.T.reshape(small_s.shape)
        share = ShareSmall(plan, me, small_s, small_box, small_part, small_box2, ssend, srecv)
        share.begin()
        for phase in range(min(final, steps2 - 1), final + 1):
            for part in late:
                scatter.advance(part, phase)
            if phase == final - 1:
                share.middle()
        o_small[...] = share.end()
        for part, out in zip(parts, (o_in, o_in, o_in, o_out, o_up, o_down)):
            scatter.finish(part, out)
        total = sum(jnp.sum(o[...] * o[...]) for o in (o_small, o_in, o_out, o_up, o_down))
        o_norm[...] = jnp.sqrt(norm_exchange(plan, me, bit, total, mine, boxes, nsend, nrecv))


def paired_layer(plan, tokens, eig_t, counts_t, ends_t, cot, shards, mols_step):
    count, width = tokens.shape
    mols_all, lap, seq = eig_t.shape
    shard = shards[0].shape[0]
    hd = Heads(width)
    steps = mols_all // mols_step
    rows = mols_step * seq
    wide = min(WIDE, count)
    steps2 = count // wide
    across_tiles = width // LANES
    last = steps - 1
    first = lambda i: lax.min(i, last)
    second = lambda i: lax.max(i - steps, 0)
    tok2 = lambda w: pl.BlockSpec((wide, w), lambda i: (second(i), 0))
    mol = lambda a, b: pl.BlockSpec((mols_step, a, b), lambda i: (first(i), 0, 0))
    tiled = lambda n: pl.BlockSpec((n, rows, LANES), lambda i: (0, first(i), 0))
    tiled2 = lambda n: pl.BlockSpec((n, wide, LANES), lambda i: (0, second(i), 0))
    sizes = dict(plan=plan, hd=hd, mols=mols_step, wide=wide, seq=seq, steps=steps, steps2=steps2)
    vm, sm, hbm = (pl.BlockSpec(memory_space=m) for m in (pltpu.VMEM, pltpu.SMEM, pl.ANY))
    sq = (width, width)
    buf = lambda c: plan.dims + (2 * shard, c)
    f32 = lambda *shape: jax.ShapeDtypeStruct(shape, F32)
    bf = lambda *shape: jax.ShapeDtypeStruct(shape, BF)
    params = lambda cid: pltpu.CompilerParams(
        vmem_limit_bytes=VMEM_LIMIT, dimension_semantics=("arbitrary",), collective_id=cid,
        has_side_effects=True,
    )
    half = width // 2
    out, proj, lse, dmid, dmix, labt, g_out, g_up, g_down, g_vec, small_t, emb, inp, w_in = pl.pallas_call(
        functools.partial(front_kernel, **sizes),
        grid=(steps + steps2,),
        in_specs=[sm, hbm, vm, vm, tok2(width)] + [vm] * 5,
        out_specs=[tok2(width), tiled(3 * across_tiles), mol(HEADS // 2, 2 * seq), tok2(width), tiled2(across_tiles)]
        + [vm] * 6 + [hbm] * 3,
        out_shape=[bf(count, width), bf(3 * across_tiles, count, LANES), f32(mols_all, HEADS // 2, 2 * seq),
                   f32(count, width), bf(across_tiles, count, LANES), bf(mols_all, 48, seq),
                   bf(*sq), bf(*sq), bf(*sq), f32(16, width), f32(SMALL, width),
                   f32(count, width), bf(across_tiles, count, LANES), bf(*buf(3 * width))],
        scratch_shapes=[pltpu.VMEM(buf(c), BF) for c in (3 * width, width, width, width, SMALL)]
        + [pltpu.VMEM((shard, SMALL), F32)] + [pltpu.VMEM((shard, half), F32)] * 6
        + [
            pltpu.VMEM((SMALL, width), F32),
            pltpu.VMEM((hd.slots(), 16, LANES), BF),
            pltpu.VMEM((count, width), BF),
            pltpu.VMEM((count, width), F32),
            pltpu.VMEM((across_tiles, count, LANES), BF),
            pltpu.VMEM((across_tiles, count, LANES), BF),
            pltpu.VMEM((HEADS, seq, seq), BF),
            pltpu.VMEM(sq, F32), pltpu.VMEM(sq, F32), pltpu.VMEM(sq, F32),
            pltpu.VMEM((16, width), F32),
        ]
        + [pltpu.SemaphoreType.DMA((7, plan.chip_bits + 2))] * 2 + [pltpu.SemaphoreType.DMA((4,))],
        compiler_params=params(0),
        name="front",
    )(counts_t, tokens, eig_t, ends_t, cot, *shards)

    low = 1 << min(3, plan.bits)
    high = plan.count // low
    boxes = low - 1 + high - 1
    slots = [pltpu.VMEM(plan.dims[j:] + (2 * shard, half), BF) for j in range(plan.chip_bits + 1)]
    shaped = [g.reshape(buf(width)) for g in (g_out, g_up, g_down)]
    tg, *sums, norm = pl.pallas_call(
        functools.partial(back_kernel, **sizes),
        grid=(steps + steps2,),
        in_specs=[sm, tiled(3 * across_tiles), mol(HEADS // 2, 2 * seq), tiled(across_tiles), tok2(width), tok2(width),
                  tiled(across_tiles), pl.BlockSpec((wide // seq, 48, seq), lambda i: (second(i), 0, 0))] + [vm] * 6,
        out_specs=[tok2(width)] + [vm] * 6,
        out_shape=[f32(count, width), f32(shard, 3 * width), f32(shard, width), f32(shard, width), f32(shard, width),
                   f32(shard, SMALL), f32(8, LANES)],
        scratch_shapes=[
            pltpu.VMEM((hd.slots(), 16, LANES), BF),
            pltpu.VMEM((HEADS, seq, seq), BF),
            pltpu.VMEM((HEADS, seq, seq), BF),
            pltpu.VMEM((HEADS, seq, seq), BF),
            pltpu.VMEM((3 * across_tiles, count, LANES), BF),
            pltpu.VMEM((width, 3 * width), F32),
            pltpu.VMEM(buf(3 * width), BF),
            pltpu.VMEM((16, width), F32),
            pltpu.VMEM((48, width), F32),
        ]
        + slots * 6
        + [pltpu.VMEM((2 * shard, half), F32)] * 6 + [pltpu.VMEM((shard, half), F32)] * 6
        + [pltpu.SemaphoreType.DMA((6, plan.chip_bits + 2))] * 2
        + [
            pltpu.VMEM((high, low, shard, SMALL), F32),
            pltpu.VMEM((low - 1, high, shard, SMALL), F32),
            pltpu.VMEM((high, shard, SMALL), F32),
            pltpu.VMEM((max(high - 1, 1), shard, SMALL), F32),
        ]
        + [pltpu.SemaphoreType.DMA((boxes,))] * 2
        + [pltpu.VMEM((8, LANES), F32), pltpu.VMEM((boxes, 8, LANES), F32)]
        + [pltpu.SemaphoreType.DMA((boxes,))] * 2,
        compiler_params=params(1),
        name="back",
    )(counts_t, proj, lse, inp, emb, dmid, dmix, labt, w_in, small_t, g_vec, *shaped)
    return out, tg, sums, norm


def plain_front_kernel(
    counts, tokens, eig, ends, cot, w_in, w_out, w_up, w_down, small,
    out_o, proj_o, lse_o, emb_o, dmid_o, dmix_o, labt_o, gout_o, gup_o, gdown_o, gvec_o,
    small_t, masks, mixed_s, p_buf, acc_out, acc_up, acc_down, acc_vec,
    *, hd, mols, seq, steps,
):
    step = pl.program_id(0)
    width = w_in.shape[0]
    across_tiles = width // LANES
    score = hd.dim ** -0.5

    @pl.when(step == 0)
    def _():
        small_t[...] = small[...].astype(F32).T
        set_masks(hd, masks)
        acc_out[...] = jnp.zeros_like(acc_out)
        acc_up[...] = jnp.zeros_like(acc_up)
        acc_down[...] = jnp.zeros_like(acc_down)
        acc_vec[...] = jnp.zeros_like(acc_vec)

    row = lambda i: small_t[i : i + 1, :]
    iota0 = lax.broadcasted_iota(jnp.int32, (seq, seq), 0)
    iota1 = lax.broadcasted_iota(jnp.int32, (seq, seq), 1)
    token_row = lax.broadcasted_iota(jnp.int32, (1, seq), 1)
    one = lambda c: c.astype(F32).astype(BF)
    label_rows = []
    for m in range(mols):
        nodes = counts[0, step * mols + m]
        live = nodes + counts[1, step * mols + m]
        eig_f = eig[m]
        eig_low = eig_f.astype(BF)
        shift = one(jnp.logical_and(iota1 - iota0 == nodes, iota1 < live))
        halves = []
        for end in range(2):
            pick = one(iota0 == ends[m, end : end + 1, :])
            edge_lab = nn(eig_low, pick).astype(BF)
            moved = nn(edge_lab, shift)
            halves.append(jnp.where(token_row < nodes, eig_f, moved))
        is_node = (token_row < nodes).astype(F32)
        is_edge = jnp.logical_and(token_row >= nodes, token_row < live).astype(F32)
        kind = jnp.where(lax.broadcasted_iota(jnp.int32, (16, seq), 0) == 0, is_node,
                         jnp.where(lax.broadcasted_iota(jnp.int32, (16, seq), 0) == 1, is_edge, 0.0))
        lab = jnp.concatenate(halves + [kind], 0)
        labt_o[m] = lab.astype(BF)
        pad = jnp.zeros((SMALL - lab.shape[0], seq), F32)
        label_rows.append(jnp.concatenate([lab, pad], 0).T.astype(BF))
    labels = jnp.concatenate(label_rows, 0)
    embedded = tokens[...].astype(F32) + nn(labels, small_t[...].astype(BF))
    emb_o[...] = embedded
    normed, recip = layer_stats(embedded)
    input_one = (normed * row(GAIN1) + row(SHIFT1)).astype(BF)
    for part in range(3):
        cols = slice(part * width, (part + 1) * width)
        value = nn(input_one, w_in[:, cols])
        if part == 0:
            value = value + row(QBIAS)
        if part == 2:
            value = value + row(VBIAS)
        value = value.astype(BF)
        for t in range(across_tiles):
            proj_o[part * across_tiles + t] = value[:, t * LANES : (t + 1) * LANES]

    for m in range(mols):
        nodes = counts[0, step * mols + m]
        live = nodes + counts[1, step * mols + m]
        key_live = lax.broadcasted_iota(jnp.int32, (seq, 2 * seq), 0) < live
        rows = slice(m * seq, (m + 1) * seq)
        for b in range(hd.blocks):
            base = b * hd.tiles * LANES
            get = lambda part: [proj_o[part * across_tiles + b * hd.tiles + t, rows, :] for t in range(hd.tiles)]
            q, k, v = get(0), get(1), get(2)
            for pair in range(hd.block // 2):
                scores = nt(pair_full(hd, k, pair), pair_rows(hd, masks, q, pair))
                scores = jnp.where(key_live, scores, MASK_FILL)
                top = jnp.max(scores, 0, keepdims=True)
                ex = jnp.exp2((scores - top) * (score * LOG2E))
                total = jnp.sum(ex, 0, keepdims=True)
                shares = (ex * (1.0 / total)).astype(BF)
                lse_o[m, b * (hd.block // 2) + pair : b * (hd.block // 2) + pair + 1, :] = (
                    top + jnp.log2(total) * (1.0 / (score * LOG2E))
                )
                for i in range(2):
                    h = 2 * pair + i
                    p_buf[b * hd.block + h] = shares[:, i * seq : (i + 1) * seq].T
            for t in range(hd.tiles):
                hs = hd.heads_of(t)
                mixed = nn(across([p_buf[b * hd.block + h] for h in hs]), tile_rows(hd, masks, v[t], t))
                mixed_s[b * hd.tiles + t, rows, :] = mixed.astype(BF)

    mixed = across([mixed_s[t] for t in range(across_tiles)])
    middle = embedded + (nt(mixed, w_out[...]) + row(OBIAS))
    normed2, recip2 = layer_stats(middle)
    input_two = (normed2 * row(GAIN2) + row(SHIFT2)).astype(BF)
    pre = nn(input_two, w_up[...]) + row(UBIAS)
    half_erf = 0.5 * (1.0 + lax.erf(pre * SQRT_HALF))
    act = (pre * half_erf).astype(BF)
    slope = half_erf + pre * jnp.exp(-0.5 * pre * pre) * INV_SQRT_TWO_PI
    out_o[...] = (middle + (nt(act, w_down[...]) + row(DBIAS))).astype(BF)
    back = cot[...]
    back_f = back.astype(F32)
    d_pre_f = nn(back, w_down[...]) * slope
    d_pre = d_pre_f.astype(BF)
    acc_down[...] += tn(back, act)
    acc_up[...] += tn(input_two, d_pre)
    d_in2 = nt(d_pre, w_up[...])
    d_mid = back_f + norm_back(d_in2, normed2, recip2, row(GAIN2))
    dmid_o[...] = d_mid
    branch = d_mid.astype(BF)
    acc_out[...] += tn(branch, mixed)
    d_mixed = nn(branch, w_out[...]).astype(BF)
    for t in range(across_tiles):
        dmix_o[t] = d_mixed[:, t * LANES : (t + 1) * LANES]
    add = lambda v: jnp.sum(v, 0, keepdims=True)
    sums = {
        OBIAS: add(branch.astype(F32)),
        GAIN2: add(d_in2 * normed2),
        SHIFT2: add(d_in2),
        UBIAS: add(d_pre.astype(F32)),
        DBIAS: add(back_f),
    }
    for i, v in sums.items():
        acc_vec[i - 34 : i - 33, :] += v

    @pl.when(step == steps - 1)
    def _():
        gout_o[...] = acc_out[...].astype(BF)
        gup_o[...] = acc_up[...].astype(BF)
        gdown_o[...] = acc_down[...].astype(BF)
        gvec_o[...] = acc_vec[...]


def plain_back_kernel(
    counts, proj, lse, emb, dmid, dmix, labt, w_in, small, gvec,
    tg_o, gin_o, gsmall_o,
    small_t, masks, pt_buf, dst_buf, ds_buf, dproj_s, acc_in, acc_vec, acc_lab,
    *, hd, mols, seq, steps,
):
    step = pl.program_id(0)
    width = w_in.shape[0]
    across_tiles = width // LANES
    score = hd.dim ** -0.5

    @pl.when(step == 0)
    def _():
        small_t[...] = small[...].astype(F32).T
        set_masks(hd, masks)
        acc_in[...] = jnp.zeros_like(acc_in)
        acc_vec[...] = gvec[...]
        acc_lab[...] = jnp.zeros_like(acc_lab)

    row = lambda i: small_t[i : i + 1, :]
    for m in range(mols):
        nodes = counts[0, step * mols + m]
        live = nodes + counts[1, step * mols + m]
        key_live = lax.broadcasted_iota(jnp.int32, (seq, 2 * seq), 0) < live
        rows = slice(m * seq, (m + 1) * seq)
        for b in range(hd.blocks):
            base = b * hd.tiles * LANES
            get = lambda ref, part: [ref[part * across_tiles + b * hd.tiles + t, rows, :] for t in range(hd.tiles)]
            q, k, v, do = get(proj, 0), get(proj, 1), get(proj, 2), get(dmix, 0)
            for pair in range(hd.block // 2):
                scores = nt(pair_full(hd, k, pair), pair_rows(hd, masks, q, pair))
                scores = jnp.where(key_live, scores, MASK_FILL)
                at = b * (hd.block // 2) + pair
                p = jnp.exp2((scores - lse[m, at : at + 1, :]) * (score * LOG2E))
                dp = nt(pair_full(hd, v, pair), pair_rows(hd, masks, do, pair))
                inner = jnp.sum(p * dp, 0, keepdims=True)
                ds = (p * (dp - inner)).astype(BF)
                p = p.astype(BF)
                for i in range(2):
                    h = b * hd.block + 2 * pair + i
                    pt_buf[h] = p[:, i * seq : (i + 1) * seq]
                    dst_buf[h] = ds[:, i * seq : (i + 1) * seq]
                    ds_buf[h] = ds[:, i * seq : (i + 1) * seq].T
            for t in range(hd.tiles):
                hs = [b * hd.block + h for h in hd.heads_of(t)]
                at = b * hd.tiles + t
                d_v = nn(across([pt_buf[h] for h in hs]), tile_rows(hd, masks, do[t], t))
                d_k = nn(across([dst_buf[h] for h in hs]), tile_rows(hd, masks, q[t], t)) * score
                d_q = nn(across([ds_buf[h] for h in hs]), tile_rows(hd, masks, k[t], t)) * score
                dproj_s[at, rows, :] = d_q.astype(BF)
                dproj_s[across_tiles + at, rows, :] = d_k.astype(BF)
                dproj_s[2 * across_tiles + at, rows, :] = d_v.astype(BF)

    normed, recip = layer_stats(emb[...])
    input_one = (normed * row(GAIN1) + row(SHIFT1)).astype(BF)
    d_proj = across([dproj_s[t] for t in range(3 * across_tiles)])
    acc_in[...] += tn(input_one, d_proj)
    d_in1 = nt(d_proj, w_in[...])
    tg = dmid[...] + norm_back(d_in1, normed, recip, row(GAIN1))
    tg_o[...] = tg
    tg_hi = tg.astype(BF)
    tg_lo = (tg - tg_hi.astype(F32)).astype(BF)
    lab = jnp.concatenate([labt[m] for m in range(mols)], 1)
    acc_lab[...] += nn(lab, tg_hi)
    acc_lab[32:48, :] += nn(lab[32:48, :], tg_lo)
    add = lambda v: jnp.sum(v, 0, keepdims=True)
    sums = {
        GAIN1: add(d_in1 * normed),
        SHIFT1: add(d_in1),
        QBIAS: add(d_proj[:, :width].astype(F32)),
        VBIAS: add(d_proj[:, 2 * width :].astype(F32)),
    }
    for i, v in sums.items():
        acc_vec[i - 34 : i - 33, :] += v

    @pl.when(step == steps - 1)
    def _():
        gin_o[...] = acc_in[...].astype(BF)
        full = jnp.concatenate(
            [acc_lab[0:32, :], acc_lab[32:34, :], acc_vec[0:9, :], jnp.zeros((SMALL - 43, width), F32)], 0
        )
        gsmall_o[...] = full.T.astype(BF)


def whole(shape):
    return pl.BlockSpec(shape, lambda *_: (0,) * len(shape), pipeline_mode=pl.Buffered(1))


def out_whole(shape):
    return pl.BlockSpec(shape, lambda *_: (0,) * len(shape))


def plain_layer(tokens, eig_t, counts_t, ends_t, cot, w_in, w_out, w_up, w_down, small, mols_step):
    count, width = tokens.shape
    mols_all, lap, seq = eig_t.shape
    hd = Heads(width)
    steps = mols_all // mols_step
    rows = mols_step * seq
    tok = lambda w: pl.BlockSpec((rows, w), lambda i, *_: (i, 0))
    tiled = lambda n: pl.BlockSpec((n, rows, LANES), lambda i, *_: (0, i, 0))
    across_tiles = width // LANES
    mol = lambda a, b: pl.BlockSpec((mols_step, a, b), lambda i, *_: (i, 0, 0))
    params = pltpu.CompilerParams(vmem_limit_bytes=VMEM_LIMIT, dimension_semantics=("arbitrary",))
    sq = (width, width)
    front = pl.pallas_call(
        functools.partial(plain_front_kernel, hd=hd, mols=mols_step, seq=seq, steps=steps),
        grid_spec=pltpu.PrefetchScalarGridSpec(
            num_scalar_prefetch=1,
            grid=(steps,),
            in_specs=[tok(width), mol(lap, seq), mol(2, seq), tok(width), whole((width, 3 * width)),
                      whole(sq), whole(sq), whole(sq), whole((width, SMALL))],
            out_specs=[tok(width), tiled(3 * across_tiles), mol(HEADS // 2, 2 * seq), tok(width), tok(width), tiled(across_tiles),
                       mol(48, seq), out_whole(sq), out_whole(sq), out_whole(sq), out_whole((16, width))],
            scratch_shapes=[
                pltpu.VMEM((SMALL, width), F32),
                pltpu.VMEM((hd.slots(), 16, LANES), BF),
                pltpu.VMEM((across_tiles, rows, LANES), BF),
                pltpu.VMEM((HEADS, seq, seq), BF),
                pltpu.VMEM(sq, F32), pltpu.VMEM(sq, F32), pltpu.VMEM(sq, F32),
                pltpu.VMEM((16, width), F32),
            ],
        ),
        out_shape=[
            jax.ShapeDtypeStruct((count, width), BF),
            jax.ShapeDtypeStruct((3 * across_tiles, count, LANES), BF),
            jax.ShapeDtypeStruct((mols_all, HEADS // 2, 2 * seq), F32),
            jax.ShapeDtypeStruct((count, width), F32),
            jax.ShapeDtypeStruct((count, width), F32),
            jax.ShapeDtypeStruct((across_tiles, count, LANES), BF),
            jax.ShapeDtypeStruct((mols_all, 48, seq), BF),
            jax.ShapeDtypeStruct(sq, BF),
            jax.ShapeDtypeStruct(sq, BF),
            jax.ShapeDtypeStruct(sq, BF),
            jax.ShapeDtypeStruct((16, width), F32),
        ],
        compiler_params=params,
        name="plain_front",
    )(counts_t, tokens, eig_t, ends_t, cot, w_in, w_out, w_up, w_down, small)
    out, proj, lse, emb, dmid, dmix, labt, g_out, g_up, g_down, g_vec = front
    tg, g_in, g_small = pl.pallas_call(
        functools.partial(plain_back_kernel, hd=hd, mols=mols_step, seq=seq, steps=steps),
        grid_spec=pltpu.PrefetchScalarGridSpec(
            num_scalar_prefetch=1,
            grid=(steps,),
            in_specs=[tiled(3 * across_tiles), mol(HEADS // 2, 2 * seq), tok(width), tok(width), tiled(across_tiles), mol(48, seq),
                      whole((width, 3 * width)), whole((width, SMALL)), whole((16, width))],
            out_specs=[tok(width), out_whole((width, 3 * width)), out_whole((width, SMALL))],
            scratch_shapes=[
                pltpu.VMEM((SMALL, width), F32),
                pltpu.VMEM((hd.slots(), 16, LANES), BF),
                pltpu.VMEM((HEADS, seq, seq), BF),
                pltpu.VMEM((HEADS, seq, seq), BF),
                pltpu.VMEM((HEADS, seq, seq), BF),
                pltpu.VMEM((3 * across_tiles, rows, LANES), BF),
                pltpu.VMEM((width, 3 * width), F32),
                pltpu.VMEM((16, width), F32),
                pltpu.VMEM((48, width), F32),
            ],
        ),
        out_shape=[
            jax.ShapeDtypeStruct((count, width), F32),
            jax.ShapeDtypeStruct((width, 3 * width), BF),
            jax.ShapeDtypeStruct((width, SMALL), BF),
        ],
        compiler_params=params,
        name="plain_back",
    )(counts_t, proj, lse, emb, dmid, dmix, labt, w_in, small, g_vec)
    return out, tg, g_in, g_out, g_up, g_down, g_small


def update_kernel(
    steps, rates, large_a, large_b, norm, g_in, g_out, g_up, g_down, g_small, *refs,
):
    states, outs, norm_o = refs[:18], refs[18:42], refs[42]
    moves = []
    for i, (source, target, stay) in enumerate(((large_b, refs[44], refs[46]), (large_a, refs[43], refs[45]))):
        size = source.shape[0] // MOVES
        for j in range(MOVES):
            part = pl.ds(j * size, size)
            moves.append((
                pltpu.make_async_copy(source.at[part], stay.at[part], refs[47].at[2 * (MOVES * i + j)]),
                pltpu.make_async_copy(stay.at[part], target.at[part], refs[47].at[2 * (MOVES * i + j) + 1]),
            ))
    for load, _ in moves:
        load.start()
    for load, store in moves:
        load.wait()
        store.start()
    norm_o[0, 0] = norm[0, 0]
    total = norm[0:1, 0:1]
    factor = jnp.minimum(1.0, CLIP_LIMIT / (total + NORM_EPS))
    t = jnp.full((1, 1), steps[0].astype(F32), F32)
    rate = rates[0]
    fix_one = 1.0 / (1.0 - jnp.exp(t * math.log(BETA_ONE)))
    fix_two = 1.0 / (1.0 - jnp.exp(t * math.log(BETA_TWO)))
    small = g_small[...]
    turned = jnp.concatenate([small, jnp.zeros((LANES - small.shape[0], SMALL), F32)], 0).T
    vec = turned[32:43, : small.shape[0]]
    vec = jnp.concatenate([vec[2:, :], vec[:2, :]], 0)
    grads = (g_in[...], g_out[...], g_up[...], g_down[...], small[:, :32], vec)
    for i, g in enumerate(grads):
        master, first, second = (states[3 * i + j][...] for j in range(3))
        g = g * factor
        first = BETA_ONE * first + (1.0 - BETA_ONE) * g
        second = BETA_TWO * second + (1.0 - BETA_TWO) * g * g
        change = first * fix_one / (jnp.sqrt(second * fix_two) + ADAM_EPS)
        if i < 5:
            change = change + DECAY_RATE * master
        for j, v in enumerate((g, first, second, master - rate * change)):
            outs[4 * i + j][...] = v
    for _, store in moves:
        store.wait()


def update_call(step_count, learn_rate, large, norm, grads, states):
    vm, sm, hbm = (pl.BlockSpec(memory_space=m) for m in (pltpu.VMEM, pltpu.SMEM, pl.ANY))
    shapes = [jax.ShapeDtypeStruct(states[3 * i].shape, F32) for i in range(6) for _ in range(4)]
    return pl.pallas_call(
        update_kernel,
        in_specs=[sm, sm, hbm, hbm] + [vm] * 24,
        out_specs=[vm] * 24 + [sm, hbm, hbm],
        out_shape=shapes + [jax.ShapeDtypeStruct((1, 1), F32)] + [jax.ShapeDtypeStruct(v.shape, v.dtype) for v in large],
        scratch_shapes=[pltpu.VMEM(v.shape, v.dtype) for v in large] + [pltpu.SemaphoreType.DMA((4 * MOVES,))],
        compiler_params=pltpu.CompilerParams(vmem_limit_bytes=VMEM_LIMIT),
        name="update",
    )(step_count.reshape(1), learn_rate.reshape(1), *large, norm, *grads, *states)


def body(
    count,
    tokens, eigvecs, counts, endpoints, cotangent,
    attend_in, attend_in_first, attend_in_second,
    attend_out, attend_out_first, attend_out_second,
    feed_up, feed_up_first, feed_up_second,
    feed_down, feed_down_first, feed_down_second,
    label_in, label_in_first, label_in_second,
    vectors, vectors_first, vectors_second,
    step_count, learn_rate,
):
    shard, width = feed_up.shape
    small_shard = jnp.concatenate(
        [label_in.T, vectors[9:].T, vectors[:9].T, jnp.zeros((shard, SMALL - 43), F32)], 1
    )
    shards = (attend_in, attend_out.T, feed_up, feed_down.T, small_shard)
    arrays = (tokens, jnp.swapaxes(eigvecs, 1, 2), counts.T, jnp.swapaxes(endpoints, 1, 2), cotangent)
    if Plan.fits(count, shard):
        out, tg, sums, norm = paired_layer(Plan(count), *arrays, shards, MOLS_STEP)
    else:
        weights = [lax.all_gather(v.astype(BF), "dp", axis=0, tiled=True) for v in shards]
        out, tg, *grads = plain_layer(*arrays, *weights, MOLS_STEP)
        sums = [lax.psum_scatter(v.astype(F32), "dp", scatter_dimension=0, tiled=True) for v in grads]
        squares = lax.psum(sum(jnp.sum(v * v) for v in sums), "dp")
        norm = jnp.full((8, LANES), jnp.sqrt(squares), F32)
    states = (
        attend_in, attend_in_first, attend_in_second,
        attend_out.T, attend_out_first.T, attend_out_second.T,
        feed_up, feed_up_first, feed_up_second,
        feed_down.T, feed_down_first.T, feed_down_second.T,
        label_in.T, label_in_first.T, label_in_second.T,
        vectors, vectors_first, vectors_second,
    )
    *new, norm, out, tg = update_call(step_count, learn_rate, (out, tg), norm, sums, states)
    new = [v.T if i // 4 in (1, 3, 4) else v for i, v in enumerate(new)]
    return (out, tg, norm.reshape(()), *new)


MOLS_STEP = 2
WIDE = 512
MOVES = 8


def solution(mesh):
    rows, cols = P("dp", None), P(None, "dp")
    state = (rows,) * 3 + (cols,) * 3 + (rows,) * 3 + (cols,) * 9
    placed = (rows, P("dp", None, None), rows, P("dp", None, None), rows) + state + (P(), P())
    results = (rows,) * 4 + (cols,) * 4 + (rows,) * 4 + (cols,) * 12
    return jax.shard_map(
        functools.partial(body, mesh.shape["dp"]),
        mesh=mesh, in_specs=placed, out_specs=(rows, rows, P()) + results, check_vma=False,
    )
```

time: 248 us -> 214 us (0.86)
  Pallas kernels: 242 us -> 208 us
    pallas_call x5 -> x3, Pallas kernels: 242 us -> 208 us  [the longest x1 101 us: paired_layer(): pl.pallas_call(functools.partial(front_kernel, **sizes), grid=(steps + st...]
where the time goes in v2:
time: 214 us; the launch traced here: 213 us
  Pallas kernels  208 us (97%)
  between operations  2.14 us (1%)
    pallas_call x1, Pallas kernels, paired_layer(): pl.pallas_call(functools.partial(front_kernel, **sizes), grid=(steps + st...  101 us
    pallas_call x1, Pallas kernels, paired_layer(): pl.pallas_call(functools.partial(back_kernel, **sizes), grid=(steps + ste...  97.3 us
    pallas_call x1, Pallas kernels, update_call(): pl.pallas_call(update_kernel, in_specs=[sm, sm, hbm, hbm] + [vm] * 24, ou...  10.1 us

profile of v2, /device:TPU:0, one launch (start us, length us, event | category | flops | bytes accessed | tf_op | source)
XLA Modules:
  0.0 213.2 jit_solution(1324180389346570032)
XLA Ops:
  0.7 0.7 slice.6
  1.4 0.1 copy.54
  1.4 0.8 copy.55
  2.2 0.1 pad.3.clone
  2.3 1.4 maximum_maximum_fusion.refs_9_
  3.7 100.7 %front.1 = (bf16[2048,768]{1,0:T(8,128)(2,1)}, bf16[18,2048,128]{2,1,0:T(8,128)(2,1)}, f32[16,16,256]{2,1,0:T(8,128)}, f32[2048,768]{1,0:T(8,128)}, bf16[6,2048,...) custom-call(s32[2,16]{1,0:T(2,128)} %bitcast.55, ...), custom_call_target="tpu_custom_call" | custom-call | tf_op jit(solution)/shard_map/front/pallas_call | solution.py:757
  104.4 97.3 %back.1 = (f32[2048,768]{1,0:T(8,128)}, f32[24,2304]{1,0:T(8,128)}, f32[24,768]{1,0:T(8,128)}, f32[24,768]{1,0:T(8,128)}, f32[24,768]{1,0:T(8,128)}, /*index=5*/f32[24,128]{1,0:T(8,128)}, f32[8,128]{1,0:T(8,128)}) custom-call(s32[2,16]{1,0:T(2,128)} %bitcast.56, bf16[18,2048,128]{2,1,0:T(8,128)(2,1)} %get-tuple-element.76.refs_1_, ...), custom_call_target="tpu_custom_call" | custom-call | tf_op jit(solution)/shard_map/back/pallas_call | solution.py:790
  203.0 10.1 %update.1 = (f32[24,2304]{1,0:T(8,128)}, f32[24,2304]{1,0:T(8,128)}, f32[24,2304]{1,0:T(8,128)}, f32[24,2304]{1,0:T(8,128)}, f32[24,768]{1,0:T(8,128)}, /*index=...) custom-call(s32[1]{0:T(128)} %bitcast.33.steps, ...), custom_call_target="tpu_custom_call" | custom-call | tf_op jit(solution)/shard_map/update/pallas_call | solution.py:1175
  (1 shorter events, 0.0 us)

commit v3 on v2

--- a/solution.py
+++ b/solution.py
@@ -93,6 +93,10 @@
 def masked(value, mask):
     rows = value.shape[0]
     return (value.reshape(rows // 16, 16, LANES) * mask[None]).reshape(rows, LANES)
+
+
+def dense(value):
+    return value.astype(F32).astype(BF)
 
 
 def set_masks(hd, masks):
@@ -126,6 +130,11 @@
 
 def tile_rows(hd, masks, tile_value, tile):
     return jnp.concatenate([masked(tile_value, masks[hd.slot(tile, h)]) for h in hd.heads_of(tile)], 0)
+
+
+def units(width):
+    unit = 2 * LANES
+    return [(at, unit) for at in range(0, width, unit)]
 
 
 class Plan:
@@ -281,11 +290,10 @@
                 mine = part["src"][...]
         else:
             mine = part["slots"][phase - 1][self.index(part, phase, True)]
-        total = mine.astype(F32) + slot[...].astype(F32)
         if phase == plan.chip_bits:
-            part["sum"][...] = total
+            part["sum"][...] = mine.astype(F32) + slot[...].astype(F32)
         else:
-            slot[...] = total.astype(BF)
+            slot[...] = mine + slot[...]
 
     def advance(self, part, phase):
         self.wait(part, phase)
@@ -303,41 +311,23 @@
         out[:, self.cols(part, False)] = part["last"][...]
 
 
-def norm_exchange(plan, me, bit, squares, mine, boxes, send, recv):
-    low = 1 << min(3, plan.bits)
-    value = jnp.full((8, LANES), squares, F32)
-    base = 0
-    for span, stride in ((low, 1), (plan.count // low, low)):
-        if span == 1:
-            continue
-        place = lax.rem(lax.div(me, jnp.int32(stride)), jnp.int32(span))
-        mine[...] = value
-        copies = []
-        for d in range(1, span):
-            to_place = lax.rem(place + d, jnp.int32(span))
-            to = me + (to_place - place) * stride
-            copies.append(pltpu.make_async_remote_copy(
-                src_ref=mine, dst_ref=boxes.at[base + d - 1], send_sem=send.at[base + d - 1],
-                recv_sem=recv.at[base + d - 1], device_id=(to,), device_id_type=MESH,
-            ))
-        for c in copies:
-            c.start()
-        for c in copies:
-            c.wait()
-        for d in range(1, span):
-            value = value + boxes[base + d - 1]
-        base += span - 1
-    return value
+def norm_exchange(plan, me, squares, mine, boxes, send, recv):
+    mine[...] = jnp.full((8, LANES), squares, F32)
+    copies = []
+    for d in range(1, plan.count):
+        copies.append(pltpu.make_async_remote_copy(
+            src_ref=mine, dst_ref=boxes.at[d - 1], send_sem=send.at[d - 1], recv_sem=recv.at[d - 1],
+            device_id=(lax.rem(me + d, jnp.int32(plan.count)),), device_id_type=MESH,
+        ))
+    for c in copies:
+        c.start()
+    for c in copies:
+        c.wait()
+    return mine[...] + jnp.sum(boxes[...], 0)
 
 
 def ring_partners(plan, me):
-    low = 1 << min(3, plan.bits)
-    found = []
-    for span, stride in ((low, 1), (plan.count // low, low)):
-        place = lax.rem(lax.div(me, jnp.int32(stride)), jnp.int32(span))
-        for d in range(1, span):
-            found.append(me + (lax.rem(place + d, jnp.int32(span)) - place) * stride)
-    return found
+    return [lax.rem(me + d, jnp.int32(plan.count)) for d in range(1, plan.count)]
 
 
 def mat(ref, *cols):
@@ -349,13 +339,13 @@
     refs = list(refs)
     take = lambda k: [refs.pop(0) for _ in range(k)]
     counts, tokens, eig, ends, cot = take(5)
-    shards = take(5)
+    s_in, s_out, s_up, s_down, label_t, vec = take(6)
     out_o, proj_o, lse_o, dmid_o, dmix_o, labt_o, gout_o, gup_o, gdown_o, gvec_o, smallt_o, emb_o, inp_o, win_o = take(14)
     w_in, w_out, w_up, w_down, small = take(5)
-    stages = take(7)
+    stages = take(1 + 6 * len(units(hd.dim * HEADS)))
     small_t, masks, tok_s, emb_s, inp_s, mixed_s, p_buf, acc_out, acc_up, acc_down, acc_vec = take(11)
     send, recv, keep = take(3)
-    s_in, s_out, s_up, s_down, s_small = shards
+    s_small, vec_s = take(2)
     step = pl.program_id(0)
     width = w_out.shape[-1]
     across_tiles = width // LANES
@@ -366,17 +356,12 @@
     make = lambda i, src, buf, at, wide, split, t: dict(
         i=i, src=src, buf=buf, stage=stages[i], at=at, width=wide, split=split, turn=t
     )
-    early = [
-        make(0, s_small, small, 0, SMALL, False, 0),
-        make(1, s_in, w_in, 0, width, True, 0),
-        make(2, s_in, w_in, width, width, True, 1),
-        make(3, s_in, w_in, 2 * width, width, True, 2),
-    ]
-    late = [
-        make(4, s_out, w_out, 0, width, True, 0),
-        make(5, s_up, w_up, 0, width, True, 1),
-        make(6, s_down, w_down, 0, width, True, 2),
-    ]
+    early = [make(0, s_small, small, 0, SMALL, False, 0)]
+    late = []
+    for src, buf, group in ((s_in, w_in, early), (s_out, w_out, late), (s_up, w_up, late), (s_down, w_down, late)):
+        for at, unit in units(buf.shape[-1]):
+            n = len(early) + len(late)
+            group.append(make(n, src, buf, at, unit, True, n))
     final = plan.chip_bits + 1
     kept = [pltpu.make_async_copy(a, b, keep.at[i]) for i, (a, b) in enumerate(((w_in, win_o), (emb_s, emb_o), (inp_s, inp_o)))]
     get_tokens = pltpu.make_async_copy(tokens, tok_s, keep.at[3])
@@ -422,6 +407,11 @@
     @pl.when(step == 0)
     def _():
         get_tokens.start()
+        vec_s[...] = jnp.zeros_like(vec_s)
+        vec_s[32:34, : vec.shape[1]] = vec[9:11, :]
+        vec_s[34:43, : vec.shape[1]] = vec[0:9, :]
+        s_small[...] = vec_s[...].T[: s_small.shape[0], :]
+        s_small[:, :32] = label_t[...]
         greet(plan, other)
         for part in early + late:
             gather.start(part, 0)
@@ -450,28 +440,15 @@
         for copy in kept:
             copy.start()
 
-    @pl.when(step < steps)
-    def _():
-        here = pl.ds(pl.multiple_of(step * rows_all, rows_all), rows_all)
-        input_one = across([inp_s[t, here, :] for t in range(across_tiles)])
-        for part in range(3):
-            value = nn(input_one, mat(w_in, slice(part * width, (part + 1) * width)))
-            if part == 0:
-                value = value + row(QBIAS)
-            if part == 2:
-                value = value + row(VBIAS)
-            value = value.astype(BF)
-            for t in range(across_tiles):
-                proj_o[part * across_tiles + t] = value[:, t * LANES : (t + 1) * LANES]
-
-        for m in range(mols):
+    def attend(some):
+        for m in some:
             nodes = counts[0, step * mols + m]
             live = nodes + counts[1, step * mols + m]
             key_live = lax.broadcasted_iota(jnp.int32, (seq, 2 * seq), 0) < live
             rows = slice(m * seq, (m + 1) * seq)
             for b in range(hd.blocks):
                 get = lambda part: [proj_o[part * across_tiles + b * hd.tiles + t, rows, :] for t in range(hd.tiles)]
-                q, k, v = get(0), get(1), get(2)
+                q, k, v = [dense(x) for x in get(0)], get(1), [dense(x) for x in get(2)]
                 for pair in range(hd.block // 2):
                     scores = nt(pair_full(hd, k, pair), pair_rows(hd, masks, q, pair))
                     scores = jnp.where(key_live, scores, MASK_FILL)
@@ -489,11 +466,37 @@
                     put = pl.ds(pl.multiple_of(step * rows_all + m * seq, seq), seq)
                     mixed_s[b * hd.tiles + t, put, :] = mixed.astype(BF)
 
-    for phase in range(1, final + 1):
-        @pl.when(step == min((1, 2, 4, 6)[min(phase, 4) - 1] + max(phase - 4, 0), steps - 1))
-        def _():
-            for part in late:
-                gather.advance(part, phase)
+    @pl.when(step < steps)
+    def _():
+        here = pl.ds(pl.multiple_of(step * rows_all, rows_all), rows_all)
+        input_one = across([inp_s[t, here, :] for t in range(across_tiles)])
+        for part in range(3):
+            value = nn(input_one, mat(w_in, slice(part * width, (part + 1) * width)))
+            if part == 0:
+                value = value + row(QBIAS)
+            if part == 2:
+                value = value + row(VBIAS)
+            value = value.astype(BF)
+            for t in range(across_tiles):
+                proj_o[part * across_tiles + t] = value[:, t * LANES : (t + 1) * LANES]
+        attend(range(mols // 2))
+
+    def pump(half):
+        for phase in range(1, final + 1):
+            slot = min(SLOTS_GATHER[min(phase, 4) - 1] + max(phase - 4, 0), 2 * steps - 1)
+            if slot % 2 == half:
+                @pl.when(step == slot // 2)
+                def _():
+                    for part in late:
+                        gather.advance(part, phase)
+
+    pump(0)
+
+    @pl.when(step < steps)
+    def _():
+        attend(range(mols // 2, mols))
+
+    pump(1)
 
     @pl.when(step >= steps)
     def _():
@@ -589,8 +592,9 @@
     tg_o, o_in, o_out, o_up, o_down, o_small, o_norm = take(7)
     masks, pt_buf, dst_buf, ds_buf, dproj_s, acc_in, g_in, acc_vec, acc_lab = take(9)
     k = plan.chip_bits + 1
-    slots = [take(k) for _ in range(6)]
-    part_sums, lasts = take(6), take(6)
+    count = 6 * len(units(hd.dim * HEADS))
+    slots = [take(k) for _ in range(count)]
+    part_sums, lasts = take(count), take(count)
     send, recv = take(2)
     small_s, small_box, small_part, small_box2, ssend, srecv = take(6)
     mine, boxes, nsend, nrecv = take(4)
@@ -601,13 +605,14 @@
     rows_all = mols * seq
     me, bit, other = my_place(plan)
     scatter = Scatter(plan, bit, other, send, recv)
-    parts = []
-    for i, (src, at, t) in enumerate([
-        (g_in, 0, 0), (g_in, width, 1), (g_in, 2 * width, 2), (g_out, 0, 0), (g_up, 0, 1), (g_down, 0, 2),
-    ]):
-        parts.append(dict(i=i, src=src, slots=slots[i], at=at, width=width, split=True, turn=t,
-                          sum=part_sums[i], last=lasts[i]))
-    late, early = parts[:3], parts[3:]
+    parts, late, early = [], [], []
+    for src, out, group in ((g_in, o_in, late), (g_out, o_out, early), (g_up, o_up, early), (g_down, o_down, early)):
+        for at, unit in units(src.shape[-1]):
+            i = len(parts)
+            part = dict(i=i, src=src, slots=slots[i], at=at, width=unit, split=True, turn=i, sum=part_sums[i],
+                        last=lasts[i], out=out)
+            parts.append(part)
+            group.append(part)
     final = plan.chip_bits + 1
 
     @pl.when(step == 0)
@@ -626,10 +631,8 @@
 
     row = lambda i: small_t[i : i + 1, :]
 
-    @pl.when(step < steps)
-    def _():
-        here = pl.ds(pl.multiple_of(step * rows_all, rows_all), rows_all)
-        for m in range(mols):
+    def attend(some):
+        for m in some:
             nodes = counts[0, step * mols + m]
             live = nodes + counts[1, step * mols + m]
             key_live = lax.broadcasted_iota(jnp.int32, (seq, 2 * seq), 0) < live
@@ -637,7 +640,8 @@
             put = pl.ds(pl.multiple_of(step * rows_all + m * seq, seq), seq)
             for b in range(hd.blocks):
                 get = lambda ref, part: [ref[part * across_tiles + b * hd.tiles + t, rows, :] for t in range(hd.tiles)]
-                q, k, v, do = get(proj, 0), get(proj, 1), get(proj, 2), get(dmix, 0)
+                q, k, v, do = [dense(x) for x in get(proj, 0)], get(proj, 1), get(proj, 2), [dense(x) for x in get(dmix, 0)]
+                k_dense = [dense(x) for x in k]
                 for pair in range(hd.block // 2):
                     scores = nt(pair_full(hd, k, pair), pair_rows(hd, masks, q, pair))
                     scores = jnp.where(key_live, scores, MASK_FILL)
@@ -657,10 +661,30 @@
                     at = b * hd.tiles + t
                     d_v = nn(across([pt_buf[h] for h in hs]), tile_rows(hd, masks, do[t], t))
                     d_k = nn(across([dst_buf[h] for h in hs]), tile_rows(hd, masks, q[t], t)) * score
-                    d_q = nn(across([ds_buf[h] for h in hs]), tile_rows(hd, masks, k[t], t)) * score
+                    d_q = nn(across([ds_buf[h] for h in hs]), tile_rows(hd, masks, k_dense[t], t)) * score
                     dproj_s[at, put, :] = d_q.astype(BF)
                     dproj_s[across_tiles + at, put, :] = d_k.astype(BF)
                     dproj_s[2 * across_tiles + at, put, :] = d_v.astype(BF)
+
+    @pl.when(step < steps)
+    def _():
+        attend(range(mols // 2))
+
+    def pump(half):
+        for phase in range(final + 1):
+            slot = min(SLOTS_SCATTER[min(phase, 4)] + max(phase - 4, 0), 2 * steps - 1)
+            if slot % 2 == half:
+                @pl.when(step == slot // 2)
+                def _():
+                    for part in early:
+                        scatter.advance(part, phase)
+
+    pump(0)
+
+    @pl.when(step < steps)
+    def _():
+        attend(range(mols // 2, mols))
+        here = pl.ds(pl.multiple_of(step * rows_all, rows_all), rows_all)
         input_one = across([inp[t] for t in range(across_tiles)])
         d_proj = across([dproj_s[t, here, :] for t in range(3 * across_tiles)])
         acc_in[...] += tn(input_one, d_proj)
@@ -668,18 +692,14 @@
         acc_vec[QBIAS - 34 : QBIAS - 33, :] += add(d_proj[:, :width].astype(F32))
         acc_vec[VBIAS - 34 : VBIAS - 33, :] += add(d_proj[:, 2 * width :].astype(F32))
 
-    for phase in range(final + 1):
-        @pl.when(step == min((0, 2, 3, 4)[min(phase, 3)] + 2 * max(phase - 3, 0), steps - 1))
-        def _():
-            for part in early:
-                scatter.advance(part, phase)
+    pump(1)
 
     @pl.when(step == steps - 1)
     def _():
         for part in late:
-            cols = slice(part["at"], part["at"] + width)
+            cols = slice(part["at"], part["at"] + part["width"])
             g_in[(slice(None),) * (plan.chip_bits + 1) + (cols,)] = acc_in[:, cols].astype(BF).reshape(
-                g_in.shape[:-1] + (width,)
+                g_in.shape[:-1] + (part["width"],)
             )
             scatter.start(part, 0)
 
@@ -720,16 +740,17 @@
             if phase == final - 1:
                 share.middle()
         o_small[...] = share.end()
-        for part, out in zip(parts, (o_in, o_in, o_in, o_out, o_up, o_down)):
-            scatter.finish(part, out)
+        for part in parts:
+            scatter.finish(part, part["out"])
         total = sum(jnp.sum(o[...] * o[...]) for o in (o_small, o_in, o_out, o_up, o_down))
-        o_norm[...] = jnp.sqrt(norm_exchange(plan, me, bit, total, mine, boxes, nsend, nrecv))
+        o_norm[...] = jnp.sqrt(norm_exchange(plan, me, total, mine, boxes, nsend, nrecv))
 
 
 def paired_layer(plan, tokens, eig_t, counts_t, ends_t, cot, shards, mols_step):
     count, width = tokens.shape
     mols_all, lap, seq = eig_t.shape
     shard = shards[0].shape[0]
+    parts = len(units(width))
     hd = Heads(width)
     steps = mols_all // mols_step
     rows = mols_step * seq
@@ -753,11 +774,10 @@
         vmem_limit_bytes=VMEM_LIMIT, dimension_semantics=("arbitrary",), collective_id=cid,
         has_side_effects=True,
     )
-    half = width // 2
     out, proj, lse, dmid, dmix, labt, g_out, g_up, g_down, g_vec, small_t, emb, inp, w_in = pl.pallas_call(
         functools.partial(front_kernel, **sizes),
         grid=(steps + steps2,),
-        in_specs=[sm, hbm, vm, vm, tok2(width)] + [vm] * 5,
+        in_specs=[sm, hbm, vm, vm, tok2(width)] + [vm] * 6,
         out_specs=[tok2(width), tiled(3 * across_tiles), mol(HEADS // 2, 2 * seq), tok2(width), tiled2(across_tiles)]
         + [vm] * 6 + [hbm] * 3,
         out_shape=[bf(count, width), bf(3 * across_tiles, count, LANES), f32(mols_all, HEADS // 2, 2 * seq),
@@ -765,7 +785,7 @@
                    bf(*sq), bf(*sq), bf(*sq), f32(16, width), f32(SMALL, width),
                    f32(count, width), bf(across_tiles, count, LANES), bf(*buf(3 * width))],
         scratch_shapes=[pltpu.VMEM(buf(c), BF) for c in (3 * width, width, width, width, SMALL)]
-        + [pltpu.VMEM((shard, SMALL), F32)] + [pltpu.VMEM((shard, half), F32)] * 6
+        + [pltpu.VMEM((shard, SMALL), F32)] + [pltpu.VMEM((shard, LANES), F32)] * (6 * parts)
         + [
             pltpu.VMEM((SMALL, width), F32),
             pltpu.VMEM((hd.slots(), 16, LANES), BF),
@@ -777,7 +797,8 @@
             pltpu.VMEM(sq, F32), pltpu.VMEM(sq, F32), pltpu.VMEM(sq, F32),
             pltpu.VMEM((16, width), F32),
         ]
-        + [pltpu.SemaphoreType.DMA((7, plan.chip_bits + 2))] * 2 + [pltpu.SemaphoreType.DMA((4,))],
+        + [pltpu.SemaphoreType.DMA((6 * parts + 1, plan.chip_bits + 2))] * 2 + [pltpu.SemaphoreType.DMA((4,))]
+        + [pltpu.VMEM((shard, SMALL), F32), pltpu.VMEM((SMALL, LANES), F32)],
         compiler_params=params(0),
         name="front",
     )(counts_t, tokens, eig_t, ends_t, cot, *shards)
@@ -785,7 +806,7 @@
     low = 1 << min(3, plan.bits)
     high = plan.count // low
     boxes = low - 1 + high - 1
-    slots = [pltpu.VMEM(plan.dims[j:] + (2 * shard, half), BF) for j in range(plan.chip_bits + 1)]
+    slots = [pltpu.VMEM(plan.dims[j:] + (2 * shard, LANES), BF) for j in range(plan.chip_bits + 1)]
     shaped = [g.reshape(buf(width)) for g in (g_out, g_up, g_down)]
     tg, *sums, norm = pl.pallas_call(
         functools.partial(back_kernel, **sizes),
@@ -806,9 +827,9 @@
             pltpu.VMEM((16, width), F32),
             pltpu.VMEM((48, width), F32),
         ]
-        + slots * 6
-        + [pltpu.VMEM((2 * shard, half), F32)] * 6 + [pltpu.VMEM((shard, half), F32)] * 6
-        + [pltpu.SemaphoreType.DMA((6, plan.chip_bits + 2))] * 2
+        + slots * (6 * parts)
+        + [pltpu.VMEM((2 * shard, LANES), F32)] * (6 * parts) + [pltpu.VMEM((shard, LANES), F32)] * (6 * parts)
+        + [pltpu.SemaphoreType.DMA((6 * parts, plan.chip_bits + 2))] * 2
         + [
             pltpu.VMEM((high, low, shard, SMALL), F32),
             pltpu.VMEM((low - 1, high, shard, SMALL), F32),
@@ -816,8 +837,8 @@
             pltpu.VMEM((max(high - 1, 1), shard, SMALL), F32),
         ]
         + [pltpu.SemaphoreType.DMA((boxes,))] * 2
-        + [pltpu.VMEM((8, LANES), F32), pltpu.VMEM((boxes, 8, LANES), F32)]
-        + [pltpu.SemaphoreType.DMA((boxes,))] * 2,
+        + [pltpu.VMEM((8, LANES), F32), pltpu.VMEM((plan.count - 1, 8, LANES), F32)]
+        + [pltpu.SemaphoreType.DMA((plan.count - 1,))] * 2,
         compiler_params=params(1),
         name="back",
     )(counts_t, proj, lse, inp, emb, dmid, dmix, labt, w_in, small_t, g_vec, *shaped)
@@ -1195,19 +1216,20 @@
     step_count, learn_rate,
 ):
     shard, width = feed_up.shape
-    small_shard = jnp.concatenate(
-        [label_in.T, vectors[9:].T, vectors[:9].T, jnp.zeros((shard, SMALL - 43), F32)], 1
-    )
-    shards = (attend_in, attend_out.T, feed_up, feed_down.T, small_shard)
+    squares = (attend_in, attend_out.T, feed_up, feed_down.T)
     arrays = (tokens, jnp.swapaxes(eigvecs, 1, 2), counts.T, jnp.swapaxes(endpoints, 1, 2), cotangent)
     if Plan.fits(count, shard):
-        out, tg, sums, norm = paired_layer(Plan(count), *arrays, shards, MOLS_STEP)
+        out, tg, sums, norm = paired_layer(Plan(count), *arrays, squares + (label_in.T, vectors), MOLS_STEP)
     else:
+        small_shard = jnp.concatenate(
+            [label_in.T, vectors[9:].T, vectors[:9].T, jnp.zeros((shard, SMALL - 43), F32)], 1
+        )
+        shards = squares + (small_shard,)
         weights = [lax.all_gather(v.astype(BF), "dp", axis=0, tiled=True) for v in shards]
-        out, tg, *grads = plain_layer(*arrays, *weights, MOLS_STEP)
+        out, tg, *grads = plain_layer(*arrays, *weights, 2)
         sums = [lax.psum_scatter(v.astype(F32), "dp", scatter_dimension=0, tiled=True) for v in grads]
-        squares = lax.psum(sum(jnp.sum(v * v) for v in sums), "dp")
-        norm = jnp.full((8, LANES), jnp.sqrt(squares), F32)
+        total = lax.psum(sum(jnp.sum(v * v) for v in sums), "dp")
+        norm = jnp.full((8, LANES), jnp.sqrt(total), F32)
     states = (
         attend_in, attend_in_first, attend_in_second,
         attend_out.T, attend_out_first.T, attend_out_second.T,
@@ -1221,7 +1243,9 @@
     return (out, tg, norm.reshape(()), *new)
 
 
-MOLS_STEP = 2
+MOLS_STEP = 4
+SLOTS_GATHER = (1, 2, 4, 6)
+SLOTS_SCATTER = (0, 2, 3, 4, 6)
 WIDE = 512
 MOVES = 8
 

time: 214 us -> 199 us (0.930)
  Pallas kernels: 208 us -> 196 us
    pallas_call x1, Pallas kernels: 97.3 us -> 89.1 us  [paired_layer(): pl.pallas_call(functools.partial(back_kernel, **sizes), grid=(steps + ste...]
    pallas_call x1, Pallas kernels: 101 us -> 97.1 us  [paired_layer(): pl.pallas_call(functools.partial(front_kernel, **sizes), grid=(steps + st...]
where the time goes in v3:
time: 199 us; the launch traced here: 198 us
  Pallas kernels  196 us (98%)
  between operations  2.14 us (1%)
    pallas_call x1, Pallas kernels, paired_layer(): pl.pallas_call(functools.partial(front_kernel, **sizes), grid=(steps + st...  97.1 us
    pallas_call x1, Pallas kernels, paired_layer(): pl.pallas_call(functools.partial(back_kernel, **sizes), grid=(steps + ste...  89.1 us
    pallas_call x1, Pallas kernels, update_call(): pl.pallas_call(update_kernel, in_specs=[sm, sm, hbm, hbm] + [vm] * 24, ou...  10.1 us

profile of v3, /device:TPU:0, one launch (start us, length us, event | category | flops | bytes accessed | tf_op | source)
XLA Modules:
  0.0 198.4 jit_solution(9664983069486451278)
XLA Ops:
  0.7 97.1 %front.1 = (bf16[2048,768]{1,0:T(8,128)(2,1)}, bf16[18,2048,128]{2,1,0:T(8,128)(2,1)}, f32[16,16,256]{2,1,0:T(8,128)}, f32[2048,768]{1,0:T(8,128)}, bf16[6,2048,...) custom-call(s32[2,16]{1,0:T(2,128)} %bitcast.49, ...), custom_call_target="tpu_custom_call" | custom-call | tf_op jit(solution)/shard_map/front/pallas_call | solution.py:777
  97.8 89.1 %back.1 = (f32[2048,768]{1,0:T(8,128)}, f32[24,2304]{1,0:T(8,128)}, f32[24,768]{1,0:T(8,128)}, f32[24,768]{1,0:T(8,128)}, f32[24,768]{1,0:T(8,128)}, /*index=5*/f32[24,128]{1,0:T(8,128)}, f32[8,128]{1,0:T(8,128)}) custom-call(s32[2,16]{1,0:T(2,128)} %bitcast.50, bf16[18,2048,128]{2,1,0:T(8,128)(2,1)} %get-tuple-element.76.refs_1_, ...), custom_call_target="tpu_custom_call" | custom-call | tf_op jit(solution)/shard_map/back/pallas_call | solution.py:811
  188.2 10.1 %update.1 = (f32[24,2304]{1,0:T(8,128)}, f32[24,2304]{1,0:T(8,128)}, f32[24,2304]{1,0:T(8,128)}, f32[24,2304]{1,0:T(8,128)}, f32[24,768]{1,0:T(8,128)}, /*index=...) custom-call(s32[1]{0:T(128)} %bitcast.30.steps, ...), custom_call_target="tpu_custom_call" | custom-call | tf_op jit(solution)/shard_map/update/pallas_call | solution.py:1196

commit v4 on v3

--- a/solution.py
+++ b/solution.py
@@ -440,7 +440,8 @@
         for copy in kept:
             copy.start()
 
-    def attend(some):
+    def attend(some, between=()):
+        between = list(between)
         for m in some:
             nodes = counts[0, step * mols + m]
             live = nodes + counts[1, step * mols + m]
@@ -460,26 +461,42 @@
                     lse_o[m, at : at + 1, :] = top + jnp.log2(total) * (1.0 / (score * LOG2E))
                     for i in range(2):
                         p_buf[b * hd.block + 2 * pair + i] = shares[:, i * seq : (i + 1) * seq].T
+                    if between and pair % EVERY == 0:
+                        between.pop(0)()
                 for t in range(hd.tiles):
                     hs = hd.heads_of(t)
                     mixed = nn(across([p_buf[b * hd.block + h] for h in hs]), tile_rows(hd, masks, v[t], t))
                     put = pl.ds(pl.multiple_of(step * rows_all + m * seq, seq), seq)
                     mixed_s[b * hd.tiles + t, put, :] = mixed.astype(BF)
+        for run in between:
+            run()
 
     @pl.when(step < steps)
     def _():
         here = pl.ds(pl.multiple_of(step * rows_all, rows_all), rows_all)
-        input_one = across([inp_s[t, here, :] for t in range(across_tiles)])
+        half = rows_all // 2
+
+        def project(n, part, cols):
+            at = pl.ds(pl.multiple_of(step * rows_all + n * half, half), half)
+            value = nn(
+                across([inp_s[t, at, :] for t in range(across_tiles)]),
+                mat(w_in, slice(part * width + cols.start, part * width + cols.stop)),
+            )
+            if part == 0:
+                value = value + small_t[QBIAS : QBIAS + 1, cols]
+            if part == 2:
+                value = value + small_t[VBIAS : VBIAS + 1, cols]
+            value = value.astype(BF)
+            for t in range((cols.stop - cols.start) // LANES):
+                tile = part * across_tiles + cols.start // LANES + t
+                proj_o[tile, n * half : (n + 1) * half, :] = value[:, t * LANES : (t + 1) * LANES]
+
         for part in range(3):
-            value = nn(input_one, mat(w_in, slice(part * width, (part + 1) * width)))
-            if part == 0:
-                value = value + row(QBIAS)
-            if part == 2:
-                value = value + row(VBIAS)
-            value = value.astype(BF)
-            for t in range(across_tiles):
-                proj_o[part * across_tiles + t] = value[:, t * LANES : (t + 1) * LANES]
-        attend(range(mols // 2))
+            project(0, part, slice(0, width))
+        later = [
+            functools.partial(project, 1, part, slice(at, at + unit)) for part in range(3) for at, unit in units(width)
+        ]
+        attend(range(mols // 2), later)
 
     def pump(half):
         for phase in range(1, final + 1):
@@ -500,39 +517,57 @@
 
     @pl.when(step >= steps)
     def _():
-        here = pl.ds(pl.multiple_of((step - steps) * wide, wide), wide)
-        mixed = across([mixed_s[t, here, :] for t in range(across_tiles)])
-        middle = emb_s[here, :] + (nt(mixed, mat(w_out)) + row(OBIAS))
-        normed2, recip2 = layer_stats(middle)
-        input_two = (normed2 * row(GAIN2) + row(SHIFT2)).astype(BF)
-        pre = nn(input_two, mat(w_up)) + row(UBIAS)
-        half_erf = 0.5 * (1.0 + lax.erf(pre * SQRT_HALF))
-        act = (pre * half_erf).astype(BF)
-        slope = half_erf + pre * jnp.exp(-0.5 * pre * pre) * INV_SQRT_TWO_PI
-        out_o[...] = (middle + (nt(act, mat(w_down)) + row(DBIAS))).astype(BF)
-        back = cot[...]
-        back_f = back.astype(F32)
-        d_pre = (nn(back, mat(w_down)) * slope).astype(BF)
-        acc_down[...] += tn(back, act)
-        acc_up[...] += tn(input_two, d_pre)
-        d_in2 = nt(d_pre, mat(w_up))
-        d_mid = back_f + norm_back(d_in2, normed2, recip2, row(GAIN2))
-        dmid_o[...] = d_mid
-        branch = d_mid.astype(BF)
-        acc_out[...] += tn(branch, mixed)
-        d_mixed = nn(branch, mat(w_out)).astype(BF)
-        for t in range(across_tiles):
-            dmix_o[t] = d_mixed[:, t * LANES : (t + 1) * LANES]
+        parts = 1
+        size = wide // parts
         add = lambda v: jnp.sum(v, 0, keepdims=True)
-        sums = {
-            OBIAS: add(branch.astype(F32)),
-            GAIN2: add(d_in2 * normed2),
-            SHIFT2: add(d_in2),
-            UBIAS: add(d_pre.astype(F32)),
-            DBIAS: add(back_f),
-        }
-        for i, v in sums.items():
-            acc_vec[i - 34 : i - 33, :] += v
+        stack = lambda vs: vs[0] if parts == 1 else jnp.concatenate(vs, 0)
+        runs = [slice(r * size, (r + 1) * size) for r in range(parts)]
+        here = [pl.ds(pl.multiple_of((step - steps) * wide + r * size, size), size) for r in range(parts)]
+        mixed = [across([mixed_s[t, h, :] for t in range(across_tiles)]) for h in here]
+        branch_in = [nt(x, mat(w_out)) for x in mixed]
+        middle, norms, inputs = [], [], []
+        for h, x in zip(here, branch_in):
+            middle.append(emb_s[h, :] + (x + row(OBIAS)))
+            norms.append(layer_stats(middle[-1]))
+            inputs.append((norms[-1][0] * row(GAIN2) + row(SHIFT2)).astype(BF))
+        acts, d_pres, backs = [], [], [cot[r, :] for r in runs]
+        for x, back in zip(inputs, backs):
+            pre = nn(x, mat(w_up)) + row(UBIAS)
+            half_erf = 0.5 * (1.0 + lax.erf(pre * SQRT_HALF))
+            acts.append((pre * half_erf).astype(BF))
+            slope = half_erf + pre * jnp.exp(-0.5 * pre * pre) * INV_SQRT_TWO_PI
+            d_pres.append((nn(back, mat(w_down)) * slope).astype(BF))
+        d_ins = [nt(x, mat(w_up)) for x in d_pres]
+        branches = []
+        totals = {i: [] for i in (OBIAS, GAIN2, SHIFT2, UBIAS, DBIAS)}
+        def close(n):
+            r, back_f, d_in2, (normed2, recip2) = runs[n], backs[n].astype(F32), d_ins[n], norms[n]
+            d_mid = back_f + norm_back(d_in2, normed2, recip2, row(GAIN2))
+            dmid_o[r, :] = d_mid
+            branches.append(d_mid.astype(BF))
+            totals[OBIAS].append(add(branches[-1].astype(F32)))
+            totals[GAIN2].append(add(d_in2 * normed2))
+            totals[SHIFT2].append(add(d_in2))
+            totals[UBIAS].append(add(d_pres[n].astype(F32)))
+            totals[DBIAS].append(add(back_f))
+        def output():
+            for r, mid, act in zip(runs, middle, acts):
+                out_o[r, :] = (mid + (nt(act, mat(w_down)) + row(DBIAS))).astype(BF)
+        def down():
+            acc_down[...] += tn(stack(backs), stack(acts))
+        def up():
+            acc_up[...] += tn(stack(inputs), stack(d_pres))
+        output()
+        close(0)
+        down()
+        up()
+        for r, x in zip(runs, branches):
+            d_mixed = nn(x, mat(w_out)).astype(BF)
+            for t in range(across_tiles):
+                dmix_o[t, r, :] = d_mixed[:, t * LANES : (t + 1) * LANES]
+        acc_out[...] += tn(stack(branches), stack(mixed))
+        for i, vs in totals.items():
+            acc_vec[i - 34 : i - 33, :] += sum(vs)
 
     @pl.when(step == steps + steps2 - 1)
     def _():
@@ -1244,9 +1279,10 @@
 
 
 MOLS_STEP = 4
-SLOTS_GATHER = (1, 2, 4, 6)
+SLOTS_GATHER = (1, 3, 4, 6)
 SLOTS_SCATTER = (0, 2, 3, 4, 6)
 WIDE = 512
+EVERY = 2
 MOVES = 8
 
 

time: 199 us -> 197 us (0.990)
  Pallas kernels: 196 us -> 194 us
where the time goes in v4:
time: 197 us
  Pallas kernels  194 us (98%)
  between operations  2.14 us (1%)
    pallas_call x1, Pallas kernels, paired_layer(): pl.pallas_call(functools.partial(front_kernel, **sizes), grid=(steps + st...  95.4 us
    pallas_call x1, Pallas kernels, paired_layer(): pl.pallas_call(functools.partial(back_kernel, **sizes), grid=(steps + ste...  89 us
    pallas_call x1, Pallas kernels, update_call(): pl.pallas_call(update_kernel, in_specs=[sm, sm, hbm, hbm] + [vm] * 24, ou...  10.1 us

profile of v4, /device:TPU:0, one launch (start us, length us, event | category | flops | bytes accessed | tf_op | source)
XLA Modules:
  0.0 196.6 jit_solution(10866119440408500239)
XLA Ops:
  0.7 95.4 %front.1 = (bf16[2048,768]{1,0:T(8,128)(2,1)}, bf16[18,2048,128]{2,1,0:T(8,128)(2,1)}, f32[16,16,256]{2,1,0:T(8,128)}, f32[2048,768]{1,0:T(8,128)}, bf16[6,2048,...) custom-call(s32[2,16]{1,0:T(2,128)} %bitcast.49, ...), custom_call_target="tpu_custom_call" | custom-call | tf_op jit(solution)/shard_map/front/pallas_call | solution.py:812
  96.0 89.0 %back.1 = (f32[2048,768]{1,0:T(8,128)}, f32[24,2304]{1,0:T(8,128)}, f32[24,768]{1,0:T(8,128)}, f32[24,768]{1,0:T(8,128)}, f32[24,768]{1,0:T(8,128)}, /*index=5*/f32[24,128]{1,0:T(8,128)}, f32[8,128]{1,0:T(8,128)}) custom-call(s32[2,16]{1,0:T(2,128)} %bitcast.50, bf16[18,2048,128]{2,1,0:T(8,128)(2,1)} %get-tuple-element.76.refs_1_, ...), custom_call_target="tpu_custom_call" | custom-call | tf_op jit(solution)/shard_map/back/pallas_call | solution.py:846
  186.3 10.1 %update.1 = (f32[24,2304]{1,0:T(8,128)}, f32[24,2304]{1,0:T(8,128)}, f32[24,2304]{1,0:T(8,128)}, f32[24,2304]{1,0:T(8,128)}, f32[24,768]{1,0:T(8,128)}, /*index=...) custom-call(s32[1]{0:T(128)} %bitcast.30.steps, ...), custom_call_target="tpu_custom_call" | custom-call | tf_op jit(solution)/shard_map/update/pallas_call | solution.py:1231

commit v5 on v4

--- a/solution.py
+++ b/solution.py
@@ -772,7 +772,7 @@
         for phase in range(min(final, steps2 - 1), final + 1):
             for part in late:
                 scatter.advance(part, phase)
-            if phase == final - 1:
+            if phase == min(final, steps2 - 1):
                 share.middle()
         o_small[...] = share.end()
         for part in parts:

time: 197 us -> 197 us (level)
  no operation moved by 1% of the time
where the time goes in v5:
time: 197 us; the launch traced here: 196 us
  Pallas kernels  194 us (98%)
  between operations  2.14 us (1%)
    pallas_call x1, Pallas kernels, paired_layer(): pl.pallas_call(functools.partial(front_kernel, **sizes), grid=(steps + st...  95.4 us
    pallas_call x1, Pallas kernels, paired_layer(): pl.pallas_call(functools.partial(back_kernel, **sizes), grid=(steps + ste...  88.9 us
    pallas_call x1, Pallas kernels, update_call(): pl.pallas_call(update_kernel, in_specs=[sm, sm, hbm, hbm] + [vm] * 24, ou...  10.1 us

profile of v5, /device:TPU:0, one launch (start us, length us, event | category | flops | bytes accessed | tf_op | source)
XLA Modules:
  0.0 196.5 jit_solution(5728098097561289817)
XLA Ops:
  0.7 95.4 %front.1 = (bf16[2048,768]{1,0:T(8,128)(2,1)}, bf16[18,2048,128]{2,1,0:T(8,128)(2,1)}, f32[16,16,256]{2,1,0:T(8,128)}, f32[2048,768]{1,0:T(8,128)}, bf16[6,2048,...) custom-call(s32[2,16]{1,0:T(2,128)} %bitcast.49, ...), custom_call_target="tpu_custom_call" | custom-call | tf_op jit(solution)/shard_map/front/pallas_call | solution.py:812
  96.0 88.9 %back.1 = (f32[2048,768]{1,0:T(8,128)}, f32[24,2304]{1,0:T(8,128)}, f32[24,768]{1,0:T(8,128)}, f32[24,768]{1,0:T(8,128)}, f32[24,768]{1,0:T(8,128)}, /*index=5*/f32[24,128]{1,0:T(8,128)}, f32[8,128]{1,0:T(8,128)}) custom-call(s32[2,16]{1,0:T(2,128)} %bitcast.50, bf16[18,2048,128]{2,1,0:T(8,128)(2,1)} %get-tuple-element.76.refs_1_, ...), custom_call_target="tpu_custom_call" | custom-call | tf_op jit(solution)/shard_map/back/pallas_call | solution.py:846
  186.2 10.1 %update.1 = (f32[24,2304]{1,0:T(8,128)}, f32[24,2304]{1,0:T(8,128)}, f32[24,2304]{1,0:T(8,128)}, f32[24,2304]{1,0:T(8,128)}, f32[24,768]{1,0:T(8,128)}, /*index=...) custom-call(s32[1]{0:T(128)} %bitcast.30.steps, ...), custom_call_target="tpu_custom_call" | custom-call | tf_op jit(solution)/shard_map/update/pallas_call | solution.py:1231
